TPU v7x, 512 devices: a whole 4x4x16 slice. The times are simulated.
512 devices in a mesh: row: 16 (over y, x_hi, core), col: 32 (over z, x_lo).
Axes of the slice: x: 4 (x_hi: 2, x_lo: 2; x = x_hi * 2 + x_lo), y: 4, z: 16, core: 2. Of those that a mesh axis runs over, the one named last changes fastest.
Arguments:
- features: bfloat16 [98304, 128], P(('col', 'row')), may hold values from -6 to 6
- weight: bfloat16 [128, 128], replicated, may hold values from -48 to 48
- block_values: bfloat16 [32768, 128, 128], P(('row', 'col')), may hold values from 0 to 1
- block_coords: int32 [32768, 2], P(('row', 'col')), may hold values from 0 to 47, as said below
- block_counts: int32 [512], P(('row', 'col')), may hold values from 1 to 64, as said below
Outputs:
- convolved: bfloat16 [98304, 128], P(('row', 'col'))
Inputs may be any that keep to these rules, and one draw needn't show every extreme that they name: `block_coords`: within one device the pairs are distinct; the first entry is below 48, the second below 24. `block_counts`: some device has exactly 64 live slots.
All inputs are finite; a program needn't handle non-finite values.
Results may differ from a plain program's by a relative error of at most 0.0049.
Values may be sent and summed in bfloat16 or wider, within the bound.
No kernel may reach another device: no remote copies, remote signals or barrier semaphores. Data moves between devices by JAX's collectives and lax.ppermute only.
A program may use at most 64 MiB of HBM per device.

v0:
```python
import jax
import jax.numpy as jnp
from jax import lax
from jax.sharding import PartitionSpec as P


def shards(features, weight, block_values, block_coords, block_counts):
    node_rows = features.shape[0]
    width = features.shape[1]
    block_slots = block_values.shape[0]
    block_size = block_values.shape[1]
    row_nodes = lax.axis_size("col") * node_rows
    col_nodes = lax.axis_size("row") * node_rows
    row_blocks = row_nodes // block_size
    col_blocks = col_nodes // block_size
    live_mask = (jnp.arange(block_slots) < block_counts[0]).astype(jnp.float32)
    row_sums = jnp.sum(block_values, axis=2, dtype=jnp.float32) * live_mask[:, None]
    col_sums = jnp.sum(block_values, axis=1, dtype=jnp.float32) * live_mask[:, None]
    row_pick = (block_coords[:, 0][:, None] == jnp.arange(row_blocks)[None, :]).astype(jnp.float32)
    col_pick = (block_coords[:, 1][:, None] == jnp.arange(col_blocks)[None, :]).astype(jnp.float32)
    row_local = jnp.dot(row_pick.T, row_sums, precision=lax.Precision.HIGHEST).reshape(row_nodes)
    col_local = jnp.dot(col_pick.T, col_sums, precision=lax.Precision.HIGHEST).reshape(col_nodes)
    col_degree = 1.0 + lax.psum_scatter(col_local, "row", scatter_dimension=0, tiled=True)
    transformed = jnp.dot(features, weight, preferred_element_type=jnp.float32)
    scaled = (transformed * lax.rsqrt(col_degree)[:, None]).astype(jnp.bfloat16)
    columns = lax.all_gather(scaled, "row", axis=0, tiled=True)
    picked = jnp.take(columns.reshape(col_blocks, block_size, width), block_coords[:, 1], axis=0)
    contrib = jnp.einsum("bij,bjf->bif", block_values, picked, preferred_element_type=jnp.float32)
    contrib = contrib * live_mask[:, None, None]
    partial_value = jnp.einsum(
        "bp,bif->pif", row_pick, contrib, precision=lax.Precision.HIGHEST
    ).reshape(row_nodes, width)
    row_degree = 1.0 + lax.psum(row_local, "col")
    source_rows = partial_value * lax.rsqrt(row_degree)[:, None]
    owned_rows = lax.psum_scatter(source_rows, "col", scatter_dimension=0, tiled=True)
    return jax.nn.relu(owned_rows).astype(jnp.bfloat16)


def solution(mesh):
    return jax.shard_map(
        shards,
        mesh=mesh,
        in_specs=(
            P(("col", "row"), None),
            P(),
            P(("row", "col"), None, None),
            P(("row", "col"), None),
            P(("row", "col")),
        ),
        out_specs=P(("row", "col"), None),
        check_vma=False,
    )
```

profile of v0, /device:TPU:24, one launch (start us, length us, event | category | flops | bytes accessed | tf_op | source)
XLA Modules:
  0.0 398.3 jit_solution(15348966052223897004)
XLA Ops:
  6.5 0.0 copy-start
  6.5 0.0 reduce-scatter.2.cloned.1.call-start
  6.5 0.7 and_bitcast_fusion
  7.2 0.8 slice_bitcast_fusion
  8.7 2.2 convert_reduce_fusion
  10.9 0.0 copy-start.1
  10.9 0.3 convolution_bitcast_fusion.1
  11.2 60.7 %all-reduce = f32[3072]{0:T(1024)S(1)} all-reduce(f32[3072]{0:T(1024)S(1)} %convolution_bitcast_fusion.1), channel_id=2, replica_groups=mesh['row'=16,'col'=32] {'row'}, use_global_device_ids=true, to_apply=%region_1.0.clone | all-reduce | flops 3072 | bytes 24576
  71.9 0.2 convolution_bitcast_fusion
  72.1 127.2 %psum.7 = f32[6144]{0:T(1024)S(1)} all-reduce(f32[6144]{0:T(1024)S(1)} %convolution_bitcast_fusion), channel_id=1, replica_groups=mesh['row'=16,'col'=32] {'col'}, use_global_device_ids=true, to_apply=%region_3.4 | all-reduce | flops 6144 | bytes 49152 | tf_op jit(solution)/shard_map/psum | solution.py:33
  199.4 1.3 dynamic-slice
  201.3 0.1 fusion.14
  201.4 0.0 copy-done
  201.4 0.9 fusion.2
  202.3 30.9 %all_gather.3 = bf16[3072,128]{1,0:T(8,128)(2,1)S(1)} all-gather(bf16[192,128]{1,0:T(8,128)(2,1)S(1)} %fusion.2), channel_id=1, replica_groups=mesh['row'=16,'col'=32] {'row'}, dimensions={0}, use_global_device_ids=true | all-gather | bytes 835584 | tf_op jit(solution)/shard_map/all_gather | solution.py:26
  233.2 2.1 gather_fusion
  235.3 5.2 %multiply_bitcast_fusion = f32[64,128,128]{1,2,0:T(8,128)} fusion(bf16[64,128,128]{2,1,0:T(8,128)(2,1)S(1)} %copy-done.1, f32[64]{0:T(128)S(1)} %compare_convert_fusion, bf16[64,128,128]{2,1,0:T(8,128)(2,1)} %gather_fusion, pred[64]{0:T(512)(128)(4,1)S(1)} %and_bitcast_fusion), kind=kOutput, calls=%fused_computation.3 | convolution fusion | flops 270532608 | bytes 8388928 | tf_op jit(solution)/shard_map/bij,bjf->bif/dot_general | solution.py:28
  240.5 5.4 %copy.10 = f32[64,128,128]{2,0,1:T(8,128)} copy(f32[64,128,128]{1,2,0:T(8,128)} %multiply_bitcast_fusion) | data formatting | bytes 8388608 | tf_op jit(solution)/shard_map/mul | solution.py:29
  245.9 4.3 %fusion.7 = f32[48,128,128]{2,0,1:T(8,128)S(1)} fusion(f32[64,128,128]{2,0,1:T(8,128)} %copy.10, s32[64]{0:T(128)S(1)} %get-tuple-element.7), kind=kOutput, calls=%fused_computation.19 | convolution fusion | flops 603982848 | bytes 7340288 | tf_op jit(solution)/shard_map/bp,bif->pif/dot_general | solution.py:30
  250.2 1.0 copy.11
  251.2 2.2 bitcast_multiply_fusion
  253.4 0.0 reduce-scatter.2.cloned.1.call-update
  253.4 136.5 %reduce-scatter.2.cloned.1.call-done = f32[192,128]{1,0:T(8,128)} async-done(((f32[6144,128]{1,0:T(8,128)}), f32[192,128]{1,0:T(8,128)}) %reduce-scatter.2.cloned.1.call-update) | async-done | bytes 98320 | tf_op jit(solution)/shard_map/reduce_scatter | solution.py:35
  389.9 1.5 maximum_convert_fusion
  (4 shorter events, 0.0 us)
Async XLA Ops:
  6.5 194.8 %copy-start = (bf16[192,128]{1,0:T(8,128)(2,1)S(1)}, bf16[192,128]{1,0:T(8,128)(2,1)}, u32[]{:S(2)}) copy-start(bf16[192,128]{1,0:T(8,128)(2,1)} %param.5) | copy-start | bytes 147460
  6.5 383.4 %reduce-scatter.2.cloned.1.call-start = ((), (), s32[]{:S(2)}) async-start(), calls=%async_computation.1 | async-start | bytes 3244032 | tf_op jit(solution)/shard_map/reduce_scatter | solution.py:35
  10.9 224.4 %copy-start.1 = (bf16[64,128,128]{2,1,0:T(8,128)(2,1)S(1)}, bf16[64,128,128]{2,1,0:T(8,128)(2,1)}, u32[]{:S(2)}) copy-start(bf16[64,128,128]{2,1,0:T(8,128)(2,1)} %param.7) | copy-start | bytes 6291460
Sparse Core Ops, SparseCore 0:
  253.5 136.3 reduce-scatter.1
where the time goes:
time: 399 us; the launch traced here: 398 us
  blocking collectives  219 us (55%)
  waiting for transfers between devices  137 us (34%)
  between operations  14.8 us (4%)
  matrix products  10.8 us (3%)
  local copies, waits for them, and re-layouts  9.85 us (2%)
  other arithmetic  7.49 us (2%)
    reduce_scatter x1, waiting for transfers between devices, shards(): lax.psum_scatter(source_rows, 'col', scatter_dimension=0, tiled=True)  137 us
    psum x1, blocking collectives, shards(): row_degree = 1.0 + lax.psum(row_local, 'col')  127 us
    unnamed x1, blocking collectives  60.7 us
    all_gather x1, blocking collectives, shards(): columns = lax.all_gather(scaled, 'row', axis=0, tiled=True)  30.9 us
  transfers between devices with their start and end apart: 1, of which 1 were waited for; matrix products, arithmetic and copies ran while one was open for 0% of the time, Pallas kernels for 0%

commit v1 on v0

v1 whole, which is shorter than its diff:
```python
import jax
import jax.numpy as jnp
from jax import lax
from jax.experimental import pallas as pl
from jax.experimental.pallas import tpu as pltpu
from jax.sharding import PartitionSpec as P

F = 128
BLK = 128
SLOTS = 64
ROW_BLOCKS = 48
COL_BLOCKS = 24
OWN = 192
N_ROW = 16
N_COL = 32
CHIPS = N_ROW // 2
NEAR = 4
FAR = N_COL // NEAR
HALF = 64
UNROLL = 8

GATHER_ROWS = OWN + 2 * COL_BLOCKS
NEAR_ROWS = FAR * OWN + 4 * FAR
FAR_ROWS = OWN + 16

CHIP_GROUPS = [[2 * m + core for m in range(CHIPS)] for core in range(2)]
NEAR_GROUPS = [[NEAR * far + near for near in range(NEAR)] for far in range(FAR)]
FAR_GROUPS = [[NEAR * far + near for far in range(FAR)] for near in range(NEAR)]

VMEM = pl.BlockSpec(memory_space=pltpu.VMEM)
SMEM = pl.BlockSpec(memory_space=pltpu.SMEM)
f32 = jnp.float32
bf16 = jnp.bfloat16


def split(value):
    high = value.astype(bf16).astype(f32)
    return high, value - high


def column_sums_kernel(counts, coords, values, features, out, sums, parts):
    sums[...] = jnp.zeros_like(sums)
    live = counts[0]

    @pl.loop(0, lax.div(live + UNROLL - 1, UNROLL))
    def _(group):
        for step in range(UNROLL):
            slot = group * UNROLL + step
            col = jnp.where(slot < live, coords[1, slot], COL_BLOCKS)
            sums[pl.ds(col, 1), :] += jnp.sum(values[slot].astype(f32), axis=0, keepdims=True)

    high, low = split(sums[:COL_BLOCKS])
    parts[:COL_BLOCKS] = high
    parts[COL_BLOCKS:] = low
    for m in range(CHIPS):
        out[m, :OWN] = features[...]
        out[m, OWN:] = parts[...].astype(bf16)


def aggregate_kernel(core, counts, coords, mine, other, weight, values, out, scales, scaled, total, row_sums):
    live = counts[0]
    sums = jnp.zeros((2 * COL_BLOCKS, BLK), f32)
    for m in range(CHIPS):
        sums += mine[m, OWN:].astype(f32) + other[m, OWN:].astype(f32)
    degree = 1.0 + (sums[:COL_BLOCKS] + sums[COL_BLOCKS:])
    scales[...] = jnp.zeros_like(scales)
    scales[:COL_BLOCKS] = lax.rsqrt(degree)
    scales[...] = scales[...].T

    def scale(pieces):
        for r in range(N_ROW):
            transformed = jnp.dot(pieces[r % 2][r // 2, :OWN], weight[...], preferred_element_type=f32)
            for part in range(OWN // HALF):
                h = r * (OWN // HALF) + part
                factor = scales[(h % 2) * HALF : (h % 2 + 1) * HALF, h // 2 : h // 2 + 1]
                rows = transformed[part * HALF : (part + 1) * HALF]
                scaled[h * HALF : (h + 1) * HALF] = (rows * factor).astype(bf16)

    @pl.when(core[0] == 0)
    def _():
        scale((mine, other))

    @pl.when(core[0] == 1)
    def _():
        scale((other, mine))

    total[...] = jnp.zeros_like(total)
    row_sums[...] = jnp.zeros_like(row_sums)
    lane = lax.broadcasted_iota(jnp.int32, (BLK, BLK), 1)

    @pl.loop(0, lax.div(live + UNROLL - 1, UNROLL))
    def _(group):
        rows, products = [], []
        sums = row_sums[...]
        for step in range(UNROLL):
            slot = group * UNROLL + step
            alive = slot < live
            row = jnp.where(alive, coords[0, slot], ROW_BLOCKS)
            col = jnp.where(alive, coords[1, slot], 0)
            picked = scaled[pl.ds(pl.multiple_of(col * BLK, BLK), BLK), :]
            block = values[slot]
            rows.append(row)
            products.append(jnp.dot(block, picked, preferred_element_type=f32))
            sums += jnp.dot(block, (lane == row).astype(f32).astype(bf16), preferred_element_type=f32)
        row_sums[...] = sums
        for row, product in zip(rows, products):
            total[pl.ds(pl.multiple_of(row * BLK, BLK), BLK), :] += product

    high, low = split(row_sums[...].T)
    for near in range(NEAR):
        for far in range(FAR):
            dest = far * NEAR + near
            out[near, far * OWN : (far + 1) * OWN] = total[dest * OWN : (dest + 1) * OWN].astype(bf16)
        picks = []
        for part in (high, low):
            for far in range(FAR):
                first = (far * NEAR + near) * OWN // BLK
                picks.append(part[first : first + 2])
        out[near, FAR * OWN :] = jnp.concatenate(picks, axis=0).astype(bf16)


def near_kernel(pieces, out):
    for far in range(FAR):
        rows = pieces[0, far * OWN : (far + 1) * OWN].astype(f32)
        for near in range(1, NEAR):
            rows += pieces[near, far * OWN : (far + 1) * OWN].astype(f32)
        out[far, :OWN] = rows.astype(bf16)
    sums = pieces[0, FAR * OWN :].astype(f32)
    for near in range(1, NEAR):
        sums += pieces[near, FAR * OWN :].astype(f32)
    high, low = split(sums[: 2 * FAR] + sums[2 * FAR :])
    for far in range(FAR):
        rows = [high[2 * far : 2 * far + 2], low[2 * far : 2 * far + 2], jnp.zeros((12, BLK), f32)]
        out[far, OWN:] = jnp.concatenate(rows, axis=0).astype(bf16)


def far_kernel(odd, pieces, out):
    rows = pieces[0].astype(f32)
    for far in range(1, FAR):
        rows += pieces[far].astype(f32)
    sums = rows[OWN : OWN + 8]
    degree = 1.0 + (sums[0:2] + sums[2:4])
    scale = jnp.concatenate([lax.rsqrt(degree), jnp.zeros((BLK - 2, BLK), f32)], axis=0).T
    halves = [scale[(h % 2) * HALF : (h % 2 + 1) * HALF, h // 2 : h // 2 + 1] for h in range(4)]
    for part in range(OWN // HALF):
        factor = jnp.where(odd[0] == 1, halves[part + 1], halves[part])
        piece = rows[part * HALF : (part + 1) * HALF] * factor
        out[part * HALF : (part + 1) * HALF] = jnp.maximum(piece, 0.0).astype(bf16)


def params():
    return pltpu.CompilerParams(vmem_limit_bytes=32 * 1024 * 1024)


def shards(features, weight, block_values, block_coords, block_counts):
    coords = block_coords.T
    core = (lax.axis_index("row") % 2).astype(jnp.int32).reshape(1)
    odd = (lax.axis_index("col") % 2).astype(jnp.int32).reshape(1)

    outgoing = pl.pallas_call(
        column_sums_kernel,
        out_shape=jax.ShapeDtypeStruct((CHIPS, GATHER_ROWS, F), bf16),
        in_specs=[SMEM, SMEM, VMEM, VMEM],
        out_specs=VMEM,
        scratch_shapes=[pltpu.VMEM((32, BLK), f32), pltpu.VMEM((2 * COL_BLOCKS, BLK), f32)],
        compiler_params=params(),
    )(block_counts, coords, block_values, features)
    mine = lax.all_to_all(outgoing, "row", 0, 0, axis_index_groups=CHIP_GROUPS, tiled=True)
    other = lax.ppermute(mine, "row", [(r, r ^ 1) for r in range(N_ROW)])

    partial = pl.pallas_call(
        aggregate_kernel,
        out_shape=jax.ShapeDtypeStruct((NEAR, NEAR_ROWS, F), bf16),
        in_specs=[SMEM, SMEM, SMEM, VMEM, VMEM, VMEM, VMEM],
        out_specs=VMEM,
        scratch_shapes=[
            pltpu.VMEM((BLK, BLK), f32),
            pltpu.VMEM((COL_BLOCKS * BLK, F), bf16),
            pltpu.VMEM(((ROW_BLOCKS + 1) * BLK, F), f32),
            pltpu.VMEM((BLK, BLK), f32),
        ],
        compiler_params=params(),
    )(core, block_counts, coords, mine, other, weight, block_values)
    partial = lax.all_to_all(partial, "col", 0, 0, axis_index_groups=NEAR_GROUPS, tiled=True)

    reduced = pl.pallas_call(
        near_kernel,
        out_shape=jax.ShapeDtypeStruct((FAR, FAR_ROWS, F), bf16),
        in_specs=[VMEM],
        out_specs=VMEM,
        compiler_params=params(),
    )(partial)
    reduced = lax.all_to_all(reduced, "col", 0, 0, axis_index_groups=FAR_GROUPS, tiled=True)

    return pl.pallas_call(
        far_kernel,
        out_shape=jax.ShapeDtypeStruct((OWN, F), bf16),
        in_specs=[SMEM, VMEM],
        out_specs=VMEM,
        compiler_params=params(),
    )(odd, reduced)


def solution(mesh):
    return jax.shard_map(
        shards,
        mesh=mesh,
        in_specs=(
            P(("col", "row"), None),
            P(),
            P(("row", "col"), None, None),
            P(("row", "col"), None),
            P(("row", "col")),
        ),
        out_specs=P(("row", "col"), None),
        check_vma=False,
    )
```

time: 399 us -> 97.1 us (0.24)
  the two profiles are of different devices: /device:TPU:24 before, /device:TPU:2 now
where the time goes in v1:
time: 97.1 us; the launch traced here: 96.7 us
  blocking collectives  40.8 us (42%)
  waiting for transfers between devices  29.4 us (30%)
  starting transfers between devices  16.5 us (17%)
  Pallas kernels  6.22 us (6%)
  local copies, waits for them, and re-layouts  3.07 us (3%)
    all_to_all x1, waiting for transfers between devices, shards(): lax.all_to_all(reduced, 'col', 0, 0, axis_index_groups=FAR_GROUPS, tiled=...  27.5 us
    all_to_all x1, blocking collectives, shards(): lax.all_to_all(partial, 'col', 0, 0, axis_index_groups=NEAR_GROUPS, tiled...  24 us
    all_to_all x1, blocking collectives, shards(): lax.all_to_all(outgoing, 'row', 0, 0, axis_index_groups=CHIP_GROUPS, tile...  16.8 us
    all_to_all x1, starting transfers between devices, shards(): lax.all_to_all(reduced, 'col', 0, 0, axis_index_groups=FAR_GROUPS, tiled=...  14.6 us
    pallas_call x1, Pallas kernels, shards(): pl.pallas_call(aggregate_kernel, out_shape=jax.ShapeDtypeStruct((NEAR, NE...  3.4 us
    unnamed x12, local copies, waits for them, and re-layouts  3.07 us
  transfers between devices with their start and end apart: 2, of which 2 were waited for; matrix products, arithmetic and copies ran while one was open for 0% of the time, Pallas kernels for 0%

profile of v1, /device:TPU:2, one launch (start us, length us, event | category | flops | bytes accessed | tf_op | source)
XLA Modules:
  0.0 96.7 jit_solution(13963752178959644299)
XLA Ops:
  0.7 0.0 copy-start
  0.7 1.6 %copy-done = bf16[64,128,128]{2,1,0:T(8,128)(2,1)S(1)} copy-done((bf16[64,128,128]{2,1,0:T(8,128)(2,1)S(1)}, bf16[64,128,128]{2,1,0:T(8,128)(2,1)}, u32[]{:S(2)}) %copy-start) | copy-done | bytes 2097176
  2.2 0.0 copy-start.2
  2.2 0.8 copy-done.2
  3.0 0.0 copy-start.4
  3.0 0.7 copy-done.4
  3.7 0.0 copy-start.1
  3.7 0.0 copy-start.3
  3.7 0.0 copy-start.5
  3.7 1.0 shard_map.55
  4.7 16.8 %all_to_all.15.mine = bf16[8,240,128]{2,1,0:T(8,128)(2,1)S(1)} all-to-all(bf16[8,240,128]{2,1,0:T(8,128)(2,1)S(1)} %shard_map.55), channel_id=1, replica_groups={{0,64,128,192,256,320,384,448},{32,96,160,224,288,352,416,480},{1,65,12..., dimensions={0} | all-to-all | bytes 983040 | tf_op jit(solution)/shard_map/all_to_all | solution.py:168
  21.5 1.9 %collective-permute-start = (bf16[8,240,128]{2,1,0:T(8,128)(2,1)S(1)}, bf16[8,240,128]{2,1,0:T(8,128)(2,1)S(1)}, u32[]{:S(2)}, u32[]{:S(2)}) collective-permute-start(bf16[8,240,128]{2,1,0:T(8,128)(2,1)S(1)} %all_to_all.15.mine), channel_id=1, source_target_pairs={{0,32},{32,0},{64,96},{96,64},{128,160},{160,128},{192,224},{224,1... | collective-permute-start | bytes 1474568 | tf_op jit(solution)/shard_map/ppermute | solution.py:169
  23.4 1.8 %collective-permute-done.other = bf16[8,240,128]{2,1,0:T(8,128)(2,1)S(1)} collective-permute-done((bf16[8,240,128]{2,1,0:T(8,128)(2,1)S(1)}, bf16[8,240,128]{2,1,0:T(8,128)(2,1)S(1)}, u32[]{:S(2)}, u32[]{:S(2)}) %collective-permute-start) | collective-permute-done | bytes 491552 | tf_op jit(solution)/shard_map/ppermute | solution.py:169
  25.2 0.0 copy-done.1
  25.2 0.0 copy-done.3
  25.2 0.0 copy-done.5
  25.2 3.4 %shard_map.56 = bf16[4,1568,128]{2,1,0:T(8,128)(2,1)S(1)} custom-call(s32[1]{0:T(128)} %bitcast.1.core, s32[1]{0:T(128)S(6)} %copy.6.counts, s32[2,64]{1,0:T(2,128)S(1)} %bitcast.4, bf16[8,240,128]{2,1,0:T(8,128)(2,1)S(1)} %all_to_all.15.mine, bf16[8,240,128]{2,1,0:T(8,128)(2,1)S(1)} %collective-permute-done.other, bf16[128,128]{1,0:T(8,128)(2,1)S(1)} %copy-done.3, ...), custom_call_target="tpu_custom_call" | custom-call | tf_op jit(solution)/shard_map/pallas_call | solution.py:171
  28.6 24.0 %all_to_all.16.pieces = bf16[4,1568,128]{2,1,0:T(8,128)(2,1)S(1)} all-to-all(bf16[4,1568,128]{2,1,0:T(8,128)(2,1)S(1)} %shard_map.56), channel_id=1, replica_groups={{0,1,2,3},{4,5,6,7},{8,9,10,11},{12,13,14,15},{16,17,18,19},{20,21,22,2..., dimensions={0} | all-to-all | bytes 3211264 | tf_op jit(solution)/shard_map/all_to_all | solution.py:184
  52.7 1.0 shard_map.57
  53.6 14.6 %all-to-all-start.2 = ((bf16[8,208,128]{2,1,0:T(8,128)(2,1)}), bf16[8,208,128]{2,1,0:T(8,128)(2,1)S(1)}, u32[]{:S(2)}, u32[]{:S(2)}) async-start(bf16[8,208,128]{2,1,0:T(8,128)(2,1)} %shard_map.57), calls=%async_computation.2 | async-start | bytes 851968 | tf_op jit(solution)/shard_map/all_to_all | solution.py:193
  68.2 27.5 %all-to-all-done.2.pieces = bf16[8,208,128]{2,1,0:T(8,128)(2,1)S(1)} async-done(((bf16[8,208,128]{2,1,0:T(8,128)(2,1)}), bf16[8,208,128]{2,1,0:T(8,128)(2,1)S(1)}, u32[]{:S(2)}, u32[]{:S(2)}) %all-to-all-start.2) | async-done | bytes 426016 | tf_op jit(solution)/shard_map/all_to_all | solution.py:193
  95.8 0.9 shard_map.58
Async XLA Ops:
  0.7 1.6 %copy-start = (bf16[64,128,128]{2,1,0:T(8,128)(2,1)S(1)}, bf16[64,128,128]{2,1,0:T(8,128)(2,1)}, u32[]{:S(2)}) copy-start(bf16[64,128,128]{2,1,0:T(8,128)(2,1)} %values.3) | copy-start | bytes 6291460
  2.2 0.8 copy-start.2
  3.0 0.7 copy-start.4
  3.7 21.5 %copy-start.1 = (bf16[64,128,128]{2,1,0:T(8,128)(2,1)S(1)}, bf16[64,128,128]{2,1,0:T(8,128)(2,1)}, u32[]{:S(2)}) copy-start(bf16[64,128,128]{2,1,0:T(8,128)(2,1)} %values.3) | copy-start | bytes 6291460
  3.7 21.5 %copy-start.3 = (bf16[128,128]{1,0:T(8,128)(2,1)S(1)}, bf16[128,128]{1,0:T(8,128)(2,1)}, u32[]{:S(2)}) copy-start(bf16[128,128]{1,0:T(8,128)(2,1)} %weight.1) | copy-start | bytes 98308
  3.7 21.5 %copy-start.5 = (s32[64,2]{0,1:T(2,128)S(1)}, s32[64,2]{0,1:T(2,128)}, u32[]{:S(2)}) copy-start(s32[64,2]{0,1:T(2,128)} %param.8) | copy-start | bytes 1540
  21.5 3.7 %collective-permute-start = (bf16[8,240,128]{2,1,0:T(8,128)(2,1)S(1)}, bf16[8,240,128]{2,1,0:T(8,128)(2,1)S(1)}, u32[]{:S(2)}, u32[]{:S(2)}) collective-permute-start(bf16[8,240,128]{2,1,0:T(8,128)(2,1)S(1)} %all_to_all.15.mine), channel_id=1, source_target_pairs={{0,32},{32,0},{64,96},{96,64},{128,160},{160,128},{192,224},{224,1... | collective-permute-start | bytes 1474568 | tf_op jit(solution)/shard_map/ppermute | solution.py:169
  53.6 42.2 %all-to-all-start.2 = ((bf16[8,208,128]{2,1,0:T(8,128)(2,1)}), bf16[8,208,128]{2,1,0:T(8,128)(2,1)S(1)}, u32[]{:S(2)}, u32[]{:S(2)}) async-start(bf16[8,208,128]{2,1,0:T(8,128)(2,1)} %shard_map.57), calls=%async_computation.2 | async-start | bytes 851968 | tf_op jit(solution)/shard_map/all_to_all | solution.py:193

commit v2 on v1

--- a/solution.py
+++ b/solution.py
@@ -21,7 +21,7 @@
 
 GATHER_ROWS = OWN + 2 * COL_BLOCKS
 NEAR_ROWS = FAR * OWN + 4 * FAR
-FAR_ROWS = OWN + 16
+FAR_ROWS = OWN + 8
 
 CHIP_GROUPS = [[2 * m + core for m in range(CHIPS)] for core in range(2)]
 NEAR_GROUPS = [[NEAR * far + near for near in range(NEAR)] for far in range(FAR)]
@@ -29,6 +29,7 @@
 
 VMEM = pl.BlockSpec(memory_space=pltpu.VMEM)
 SMEM = pl.BlockSpec(memory_space=pltpu.SMEM)
+HBM = pl.BlockSpec(memory_space=pltpu.HBM)
 f32 = jnp.float32
 bf16 = jnp.bfloat16
 
@@ -38,22 +39,40 @@
     return high, value - high
 
 
-def column_sums_kernel(counts, coords, values, features, out, sums, parts):
+def column_sums_kernel(counts_in, coords_in, values_in, features_in, out, counts, coords, values, features, sums, parts, small_sems, sems):
+    small = [
+        pltpu.make_async_copy(counts_in, counts, small_sems.at[0]),
+        pltpu.make_async_copy(coords_in, coords, small_sems.at[1]),
+        pltpu.make_async_copy(features_in, features, small_sems.at[2]),
+    ]
+    for copy in small:
+        copy.start()
+    chunks = []
+    for group in range(SLOTS // UNROLL):
+        slots = pl.ds(group * UNROLL, UNROLL)
+        chunks.append(pltpu.make_async_copy(values_in.at[slots], values.at[slots], sems.at[group]))
+        chunks[-1].start()
     sums[...] = jnp.zeros_like(sums)
+    small[2].wait()
+    for m in range(CHIPS):
+        out[m, :OWN] = features[...]
+    small[0].wait()
+    small[1].wait()
     live = counts[0]
-
-    @pl.loop(0, lax.div(live + UNROLL - 1, UNROLL))
-    def _(group):
-        for step in range(UNROLL):
-            slot = group * UNROLL + step
-            col = jnp.where(slot < live, coords[1, slot], COL_BLOCKS)
-            sums[pl.ds(col, 1), :] += jnp.sum(values[slot].astype(f32), axis=0, keepdims=True)
+    for group in range(SLOTS // UNROLL):
+        chunks[group].wait()
+
+        @pl.when(group * UNROLL < live)
+        def _():
+            for step in range(UNROLL):
+                slot = group * UNROLL + step
+                col = jnp.where(slot < live, coords[1, slot], COL_BLOCKS)
+                sums[pl.ds(col, 1), :] += jnp.sum(values[slot].astype(f32), axis=0, keepdims=True)
 
     high, low = split(sums[:COL_BLOCKS])
     parts[:COL_BLOCKS] = high
     parts[COL_BLOCKS:] = low
     for m in range(CHIPS):
-        out[m, :OWN] = features[...]
         out[m, OWN:] = parts[...].astype(bf16)
 
 
@@ -120,18 +139,17 @@
 
 
 def near_kernel(pieces, out):
-    for far in range(FAR):
-        rows = pieces[0, far * OWN : (far + 1) * OWN].astype(f32)
-        for near in range(1, NEAR):
-            rows += pieces[near, far * OWN : (far + 1) * OWN].astype(f32)
-        out[far, :OWN] = rows.astype(bf16)
     sums = pieces[0, FAR * OWN :].astype(f32)
     for near in range(1, NEAR):
         sums += pieces[near, FAR * OWN :].astype(f32)
     high, low = split(sums[: 2 * FAR] + sums[2 * FAR :])
     for far in range(FAR):
-        rows = [high[2 * far : 2 * far + 2], low[2 * far : 2 * far + 2], jnp.zeros((12, BLK), f32)]
-        out[far, OWN:] = jnp.concatenate(rows, axis=0).astype(bf16)
+        rows = pieces[0, far * OWN : (far + 1) * OWN].astype(f32)
+        for near in range(1, NEAR):
+            rows += pieces[near, far * OWN : (far + 1) * OWN].astype(f32)
+        pair = slice(2 * far, 2 * far + 2)
+        tail = jnp.concatenate([high[pair], low[pair], jnp.zeros((4, BLK), f32)], axis=0)
+        out[far] = jnp.concatenate([rows, tail], axis=0).astype(bf16)
 
 
 def far_kernel(odd, pieces, out):
@@ -148,8 +166,8 @@
         out[part * HALF : (part + 1) * HALF] = jnp.maximum(piece, 0.0).astype(bf16)
 
 
-def params():
-    return pltpu.CompilerParams(vmem_limit_bytes=32 * 1024 * 1024)
+def params(mebibytes=32):
+    return pltpu.CompilerParams(vmem_limit_bytes=mebibytes * 1024 * 1024)
 
 
 def shards(features, weight, block_values, block_coords, block_counts):
@@ -160,10 +178,19 @@
     outgoing = pl.pallas_call(
         column_sums_kernel,
         out_shape=jax.ShapeDtypeStruct((CHIPS, GATHER_ROWS, F), bf16),
-        in_specs=[SMEM, SMEM, VMEM, VMEM],
-        out_specs=VMEM,
-        scratch_shapes=[pltpu.VMEM((32, BLK), f32), pltpu.VMEM((2 * COL_BLOCKS, BLK), f32)],
-        compiler_params=params(),
+        in_specs=[HBM, HBM, HBM, HBM],
+        out_specs=VMEM,
+        scratch_shapes=[
+            pltpu.SMEM((1,), jnp.int32),
+            pltpu.SMEM((2, SLOTS), jnp.int32),
+            pltpu.VMEM((SLOTS, BLK, BLK), bf16),
+            pltpu.VMEM((OWN, F), bf16),
+            pltpu.VMEM((32, BLK), f32),
+            pltpu.VMEM((2 * COL_BLOCKS, BLK), f32),
+            pltpu.SemaphoreType.DMA((3,)),
+            pltpu.SemaphoreType.DMA((SLOTS // UNROLL,)),
+        ],
+        compiler_params=params(60),
     )(block_counts, coords, block_values, features)
     mine = lax.all_to_all(outgoing, "row", 0, 0, axis_index_groups=CHIP_GROUPS, tiled=True)
     other = lax.ppermute(mine, "row", [(r, r ^ 1) for r in range(N_ROW)])

time: 97.1 us -> 95 us (0.978)
  local copies, waits for them, and re-layouts: 3.07 us -> 0.01 us
  Pallas kernels: 6.22 us -> 7.71 us
    unnamed x12 -> x6, local copies, waits for them, and re-layouts: 3.07 us -> 0.01 us
    pallas_call x1, Pallas kernels: 0.97 us -> 2.75 us  [shards(): pl.pallas_call(column_sums_kernel, out_shape=jax.ShapeDtypeStruct((CHIPS,...]
where the time goes in v2:
time: 95 us; the launch traced here: 94.7 us
  blocking collectives  41.6 us (44%)
  waiting for transfers between devices  28.8 us (30%)
  starting transfers between devices  15.9 us (17%)
  Pallas kernels  7.71 us (8%)
    all_to_all x1, waiting for transfers between devices, shards(): lax.all_to_all(reduced, 'col', 0, 0, axis_index_groups=FAR_GROUPS, tiled=...  27 us
    all_to_all x1, blocking collectives, shards(): lax.all_to_all(partial, 'col', 0, 0, axis_index_groups=NEAR_GROUPS, tiled...  24.4 us
    all_to_all x1, blocking collectives, shards(): lax.all_to_all(outgoing, 'row', 0, 0, axis_index_groups=CHIP_GROUPS, tile...  17.1 us
    all_to_all x1, starting transfers between devices, shards(): lax.all_to_all(reduced, 'col', 0, 0, axis_index_groups=FAR_GROUPS, tiled=...  14 us
    pallas_call x1, Pallas kernels, shards(): pl.pallas_call(aggregate_kernel, out_shape=jax.ShapeDtypeStruct((NEAR, NE...  3.11 us
    pallas_call x1, Pallas kernels, shards(): pl.pallas_call(column_sums_kernel, out_shape=jax.ShapeDtypeStruct((CHIPS,...  2.75 us
    ppermute x1, starting transfers between devices, shards(): other = lax.ppermute(mine, 'row', [(r, r ^ 1) for r in range(N_ROW)])  1.91 us
  transfers between devices with their start and end apart: 2, of which 2 were waited for; matrix products, arithmetic and copies ran while one was open for 0% of the time, Pallas kernels for 0%

profile of v2, /device:TPU:2, one launch (start us, length us, event | category | flops | bytes accessed | tf_op | source)
XLA Modules:
  0.0 94.7 jit_solution(6666843212124253917)
XLA Ops:
  0.7 0.0 copy-start
  0.7 0.0 copy-start.1
  0.7 0.0 copy-start.2
  0.7 2.8 %shard_map.55 = bf16[8,240,128]{2,1,0:T(8,128)(2,1)} custom-call(s32[1]{0:T(128)S(6)} %copy.6.counts_in.counts, s32[2,64]{1,0:T(2,128)} %bitcast.3, bf16[64,128,128]{2,1,0:T(8,128)(2,1)} %values.1, bf16[192,128]{1,0:T(8,128)(2,1)} %features_in.1), custom_call_target="tpu_custom_call" | custom-call | tf_op jit(solution)/shard_map/pallas_call | solution.py:178
  3.4 17.1 %all_to_all.15.mine = bf16[8,240,128]{2,1,0:T(8,128)(2,1)S(1)} all-to-all(bf16[8,240,128]{2,1,0:T(8,128)(2,1)} %shard_map.55), channel_id=1, replica_groups={{0,64,128,192,256,320,384,448},{32,96,160,224,288,352,416,480},{1,65,12..., dimensions={0} | all-to-all | bytes 983040 | tf_op jit(solution)/shard_map/all_to_all | solution.py:195
  20.6 1.9 %collective-permute-start = (bf16[8,240,128]{2,1,0:T(8,128)(2,1)S(1)}, bf16[8,240,128]{2,1,0:T(8,128)(2,1)S(1)}, u32[]{:S(2)}, u32[]{:S(2)}) collective-permute-start(bf16[8,240,128]{2,1,0:T(8,128)(2,1)S(1)} %all_to_all.15.mine), channel_id=1, source_target_pairs={{0,32},{32,0},{64,96},{96,64},{128,160},{160,128},{192,224},{224,1... | collective-permute-start | bytes 1474568 | tf_op jit(solution)/shard_map/ppermute | solution.py:196
  22.5 1.8 %collective-permute-done.other = bf16[8,240,128]{2,1,0:T(8,128)(2,1)S(1)} collective-permute-done((bf16[8,240,128]{2,1,0:T(8,128)(2,1)S(1)}, bf16[8,240,128]{2,1,0:T(8,128)(2,1)S(1)}, u32[]{:S(2)}, u32[]{:S(2)}) %collective-permute-start) | collective-permute-done | bytes 491552 | tf_op jit(solution)/shard_map/ppermute | solution.py:196
  24.3 0.0 copy-done
  24.3 0.0 copy-done.1
  24.3 0.0 copy-done.2
  24.3 3.1 %shard_map.56 = bf16[4,1568,128]{2,1,0:T(8,128)(2,1)S(1)} custom-call(s32[1]{0:T(128)} %bitcast.1.core, s32[1]{0:T(128)S(6)} %copy.6.counts_in.counts, s32[2,64]{1,0:T(2,128)S(1)} %bitcast.4, bf16[8,240,128]{2,1,0:T(8,128)(2,1)S(1)} %all_to_all.15.mine, bf16[8,240,128]{2,1,0:T(8,128)(2,1)S(1)} %collective-permute-done.other, bf16[128,128]{1,0:T(8,128)(2,1)S(1)} %copy-done.1, ...), custom_call_target="tpu_custom_call" | custom-call | tf_op jit(solution)/shard_map/pallas_call | solution.py:198
  27.4 24.4 %all_to_all.16.pieces = bf16[4,1568,128]{2,1,0:T(8,128)(2,1)S(1)} all-to-all(bf16[4,1568,128]{2,1,0:T(8,128)(2,1)S(1)} %shard_map.56), channel_id=1, replica_groups={{0,1,2,3},{4,5,6,7},{8,9,10,11},{12,13,14,15},{16,17,18,19},{20,21,22,2..., dimensions={0} | all-to-all | bytes 3211264 | tf_op jit(solution)/shard_map/all_to_all | solution.py:211
  51.9 1.0 %shard_map.57 = bf16[8,200,128]{2,1,0:T(8,128)(2,1)} custom-call(bf16[4,1568,128]{2,1,0:T(8,128)(2,1)S(1)} %all_to_all.16.pieces), custom_call_target="tpu_custom_call" | custom-call | tf_op jit(solution)/shard_map/pallas_call | solution.py:213
  52.8 14.0 %all-to-all-start.2 = ((bf16[8,200,128]{2,1,0:T(8,128)(2,1)}), bf16[8,200,128]{2,1,0:T(8,128)(2,1)S(1)}, u32[]{:S(2)}, u32[]{:S(2)}) async-start(bf16[8,200,128]{2,1,0:T(8,128)(2,1)} %shard_map.57), calls=%async_computation.2 | async-start | bytes 819200 | tf_op jit(solution)/shard_map/all_to_all | solution.py:220
  66.8 27.0 %all-to-all-done.2.pieces = bf16[8,200,128]{2,1,0:T(8,128)(2,1)S(1)} async-done(((bf16[8,200,128]{2,1,0:T(8,128)(2,1)}), bf16[8,200,128]{2,1,0:T(8,128)(2,1)S(1)}, u32[]{:S(2)}, u32[]{:S(2)}) %all-to-all-start.2) | async-done | bytes 409632 | tf_op jit(solution)/shard_map/all_to_all | solution.py:220
  93.8 0.9 shard_map.58
Async XLA Ops:
  0.7 23.7 %copy-start = (bf16[64,128,128]{2,1,0:T(8,128)(2,1)S(1)}, bf16[64,128,128]{2,1,0:T(8,128)(2,1)}, u32[]{:S(2)}) copy-start(bf16[64,128,128]{2,1,0:T(8,128)(2,1)} %values.1) | copy-start | bytes 6291460
  0.7 23.6 %copy-start.1 = (bf16[128,128]{1,0:T(8,128)(2,1)S(1)}, bf16[128,128]{1,0:T(8,128)(2,1)}, u32[]{:S(2)}) copy-start(bf16[128,128]{1,0:T(8,128)(2,1)} %weight.1) | copy-start | bytes 98308
  0.7 23.6 %copy-start.2 = (s32[64,2]{0,1:T(2,128)S(1)}, s32[64,2]{0,1:T(2,128)}, u32[]{:S(2)}) copy-start(s32[64,2]{0,1:T(2,128)} %param.8) | copy-start | bytes 1540
  20.6 3.7 %collective-permute-start = (bf16[8,240,128]{2,1,0:T(8,128)(2,1)S(1)}, bf16[8,240,128]{2,1,0:T(8,128)(2,1)S(1)}, u32[]{:S(2)}, u32[]{:S(2)}) collective-permute-start(bf16[8,240,128]{2,1,0:T(8,128)(2,1)S(1)} %all_to_all.15.mine), channel_id=1, source_target_pairs={{0,32},{32,0},{64,96},{96,64},{128,160},{160,128},{192,224},{224,1... | collective-permute-start | bytes 1474568 | tf_op jit(solution)/shard_map/ppermute | solution.py:196
  52.8 41.0 %all-to-all-start.2 = ((bf16[8,200,128]{2,1,0:T(8,128)(2,1)}), bf16[8,200,128]{2,1,0:T(8,128)(2,1)S(1)}, u32[]{:S(2)}, u32[]{:S(2)}) async-start(bf16[8,200,128]{2,1,0:T(8,128)(2,1)} %shard_map.57), calls=%async_computation.2 | async-start | bytes 819200 | tf_op jit(solution)/shard_map/all_to_all | solution.py:220

commit v3 on v2

--- a/solution.py
+++ b/solution.py
@@ -18,6 +18,7 @@
 FAR = N_COL // NEAR
 HALF = 64
 UNROLL = 8
+BATCH = 16
 
 GATHER_ROWS = OWN + 2 * COL_BLOCKS
 NEAR_ROWS = FAR * OWN + 4 * FAR
@@ -76,7 +77,32 @@
         out[m, OWN:] = parts[...].astype(bf16)
 
 
-def aggregate_kernel(core, counts, coords, mine, other, weight, values, out, scales, scaled, total, row_sums):
+def row_sums_kernel(mine, counts, coords, values, out, sums):
+    live = counts[0]
+    sums[...] = jnp.zeros_like(sums)
+    lane = lax.broadcasted_iota(jnp.int32, (BLK, BLK), 1)
+
+    @pl.loop(0, lax.div(live + BATCH - 1, BATCH))
+    def _(group):
+        added = sums[...]
+        for step in range(BATCH):
+            slot = group * BATCH + step
+            row = jnp.where(slot < live, coords[0, slot], ROW_BLOCKS)
+            picked = (lane == row).astype(f32).astype(bf16)
+            added += jnp.dot(values[slot], picked, preferred_element_type=f32)
+        sums[...] = added
+
+    high, low = split(sums[...].T)
+    for near in range(NEAR):
+        picks = []
+        for part in (high, low):
+            for far in range(FAR):
+                first = (far * NEAR + near) * OWN // BLK
+                picks.append(part[first : first + 2])
+        out[near] = jnp.concatenate(picks, axis=0).astype(bf16)
+
+
+def aggregate_kernel(core, counts, coords, mine, other, weight, values, row_sums, out, scales, scaled, total):
     live = counts[0]
     sums = jnp.zeros((2 * COL_BLOCKS, BLK), f32)
     for m in range(CHIPS):
@@ -104,38 +130,26 @@
         scale((other, mine))
 
     total[...] = jnp.zeros_like(total)
-    row_sums[...] = jnp.zeros_like(row_sums)
-    lane = lax.broadcasted_iota(jnp.int32, (BLK, BLK), 1)
-
-    @pl.loop(0, lax.div(live + UNROLL - 1, UNROLL))
+
+    @pl.loop(0, lax.div(live + BATCH - 1, BATCH))
     def _(group):
         rows, products = [], []
-        sums = row_sums[...]
-        for step in range(UNROLL):
-            slot = group * UNROLL + step
+        for step in range(BATCH):
+            slot = group * BATCH + step
             alive = slot < live
             row = jnp.where(alive, coords[0, slot], ROW_BLOCKS)
             col = jnp.where(alive, coords[1, slot], 0)
             picked = scaled[pl.ds(pl.multiple_of(col * BLK, BLK), BLK), :]
-            block = values[slot]
             rows.append(row)
-            products.append(jnp.dot(block, picked, preferred_element_type=f32))
-            sums += jnp.dot(block, (lane == row).astype(f32).astype(bf16), preferred_element_type=f32)
-        row_sums[...] = sums
+            products.append(jnp.dot(values[slot], picked, preferred_element_type=f32))
         for row, product in zip(rows, products):
             total[pl.ds(pl.multiple_of(row * BLK, BLK), BLK), :] += product
 
-    high, low = split(row_sums[...].T)
     for near in range(NEAR):
         for far in range(FAR):
             dest = far * NEAR + near
             out[near, far * OWN : (far + 1) * OWN] = total[dest * OWN : (dest + 1) * OWN].astype(bf16)
-        picks = []
-        for part in (high, low):
-            for far in range(FAR):
-                first = (far * NEAR + near) * OWN // BLK
-                picks.append(part[first : first + 2])
-        out[near, FAR * OWN :] = jnp.concatenate(picks, axis=0).astype(bf16)
+        out[near, FAR * OWN :] = row_sums[near]
 
 
 def near_kernel(pieces, out):
@@ -195,19 +209,28 @@
     mine = lax.all_to_all(outgoing, "row", 0, 0, axis_index_groups=CHIP_GROUPS, tiled=True)
     other = lax.ppermute(mine, "row", [(r, r ^ 1) for r in range(N_ROW)])
 
+    row_sums = pl.pallas_call(
+        row_sums_kernel,
+        out_shape=jax.ShapeDtypeStruct((NEAR, 4 * FAR, BLK), bf16),
+        in_specs=[HBM, SMEM, SMEM, VMEM],
+        out_specs=VMEM,
+        scratch_shapes=[pltpu.VMEM((BLK, BLK), f32)],
+        compiler_params=params(),
+        cost_estimate=pl.CostEstimate(flops=2 * SLOTS * BLK**3, bytes_accessed=2 * SLOTS * BLK**2, transcendentals=0),
+    )(mine, block_counts, coords, block_values)
+
     partial = pl.pallas_call(
         aggregate_kernel,
         out_shape=jax.ShapeDtypeStruct((NEAR, NEAR_ROWS, F), bf16),
-        in_specs=[SMEM, SMEM, SMEM, VMEM, VMEM, VMEM, VMEM],
+        in_specs=[SMEM, SMEM, SMEM, VMEM, VMEM, VMEM, VMEM, VMEM],
         out_specs=VMEM,
         scratch_shapes=[
             pltpu.VMEM((BLK, BLK), f32),
             pltpu.VMEM((COL_BLOCKS * BLK, F), bf16),
             pltpu.VMEM(((ROW_BLOCKS + 1) * BLK, F), f32),
-            pltpu.VMEM((BLK, BLK), f32),
         ],
         compiler_params=params(),
-    )(core, block_counts, coords, mine, other, weight, block_values)
+    )(core, block_counts, coords, mine, other, weight, block_values, row_sums)
     partial = lax.all_to_all(partial, "col", 0, 0, axis_index_groups=NEAR_GROUPS, tiled=True)
 
     reduced = pl.pallas_call(

time: 95 us -> 95.4 us (level)
  waiting for transfers between devices: 28.8 us -> 27.3 us
    ppermute x1, waiting for transfers between devices: 1.82 us -> 0.26 us  [shards(): other = lax.ppermute(mine, 'row', [(r, r ^ 1) for r in range(N_ROW)])]
    pallas_call x0 -> x1, Pallas kernels: none -> 1.53 us  [shards(): pl.pallas_call(row_sums_kernel, out_shape=jax.ShapeDtypeStruct((NEAR, 4 *...]
  transfers between devices with their start and end apart: 2 -> 2, of which waited for: 2 -> 2; matrix products, arithmetic and copies ran while one was open for 0% -> 0% of each run, Pallas kernels for 0% -> 2%
where the time goes in v3:
time: 95.4 us; the launch traced here: 95 us
  blocking collectives  41.5 us (44%)
  waiting for transfers between devices  27.3 us (29%)
  starting transfers between devices  16.8 us (18%)
  Pallas kernels  8.63 us (9%)
    all_to_all x1, waiting for transfers between devices, shards(): lax.all_to_all(reduced, 'col', 0, 0, axis_index_groups=FAR_GROUPS, tiled=...  27.1 us
    all_to_all x1, blocking collectives, shards(): lax.all_to_all(partial, 'col', 0, 0, axis_index_groups=NEAR_GROUPS, tiled...  24.2 us
    all_to_all x1, blocking collectives, shards(): lax.all_to_all(outgoing, 'row', 0, 0, axis_index_groups=CHIP_GROUPS, tile...  17.3 us
    all_to_all x1, starting transfers between devices, shards(): lax.all_to_all(reduced, 'col', 0, 0, axis_index_groups=FAR_GROUPS, tiled=...  14.9 us
    pallas_call x1, Pallas kernels, shards(): pl.pallas_call(column_sums_kernel, out_shape=jax.ShapeDtypeStruct((CHIPS,...  2.75 us
    pallas_call x1, Pallas kernels, shards(): pl.pallas_call(aggregate_kernel, out_shape=jax.ShapeDtypeStruct((NEAR, NE...  2.51 us
    ppermute x1, starting transfers between devices, shards(): other = lax.ppermute(mine, 'row', [(r, r ^ 1) for r in range(N_ROW)])  1.91 us
  transfers between devices with their start and end apart: 2, of which 2 were waited for; matrix products, arithmetic and copies ran while one was open for 0% of the time, Pallas kernels for 2%

profile of v3, /device:TPU:2, one launch (start us, length us, event | category | flops | bytes accessed | tf_op | source)
XLA Modules:
  0.0 95.0 jit_solution(9286568922728434708)
XLA Ops:
  0.7 0.0 copy-start
  0.7 0.0 copy-start.2
  0.7 2.7 %shard_map.55 = bf16[8,240,128]{2,1,0:T(8,128)(2,1)} custom-call(s32[1]{0:T(128)S(6)} %copy.6.counts_in.counts, s32[2,64]{1,0:T(2,128)} %bitcast.3, bf16[64,128,128]{2,1,0:T(8,128)(2,1)} %values.3, bf16[192,128]{1,0:T(8,128)(2,1)} %features_in.1), custom_call_target="tpu_custom_call" | custom-call | tf_op jit(solution)/shard_map/pallas_call | solution.py:192
  3.4 0.0 copy-start.1
  3.4 17.3 %all_to_all.15.mine = bf16[8,240,128]{2,1,0:T(8,128)(2,1)S(1)} all-to-all(bf16[8,240,128]{2,1,0:T(8,128)(2,1)} %shard_map.55), channel_id=1, replica_groups={{0,64,128,192,256,320,384,448},{32,96,160,224,288,352,416,480},{1,65,12..., dimensions={0} | all-to-all | bytes 983040 | tf_op jit(solution)/shard_map/all_to_all | solution.py:209
  20.7 1.9 %collective-permute-start = (bf16[8,240,128]{2,1,0:T(8,128)(2,1)S(1)}, bf16[8,240,128]{2,1,0:T(8,128)(2,1)S(1)}, u32[]{:S(2)}, u32[]{:S(2)}) collective-permute-start(bf16[8,240,128]{2,1,0:T(8,128)(2,1)S(1)} %all_to_all.15.mine), channel_id=1, source_target_pairs={{0,32},{32,0},{64,96},{96,64},{128,160},{160,128},{192,224},{224,1... | collective-permute-start | bytes 1474568 | tf_op jit(solution)/shard_map/ppermute | solution.py:210
  22.6 0.0 copy-done
  22.7 0.0 copy-done.2
  22.7 1.5 %shard_map.56.row_sums = bf16[4,32,128]{2,1,0:T(8,128)(2,1)S(1)} custom-call(bf16[8,240,128]{2,1,0:T(8,128)(2,1)S(1)} %all_to_all.15.mine, s32[1]{0:T(128)S(6)} %copy.6.counts_in.counts, s32[2,64]{1,0:T(2,128)S(1)} %bitcast.4, bf16[64,128,128]{2,1,0:T(8,128)(2,1)S(1)} %copy-done), custom_call_target="tpu_custom_call" | custom-call | flops 268435456 | bytes 2097152 | tf_op jit(solution)/shard_map/pallas_call | solution.py:212
  24.2 0.3 collective-permute-done.other
  24.5 0.0 copy-done.1
  24.5 2.5 %shard_map.57 = bf16[4,1568,128]{2,1,0:T(8,128)(2,1)S(1)} custom-call(s32[1]{0:T(128)} %bitcast.1.core, s32[1]{0:T(128)S(6)} %copy.6.counts_in.counts, s32[2,64]{1,0:T(2,128)S(1)} %bitcast.5, bf16[8,240,128]{2,1,0:T(8,128)(2,1)S(1)} %all_to_all.15.mine, bf16[8,240,128]{2,1,0:T(8,128)(2,1)S(1)} %collective-permute-done.other, bf16[128,128]{1,0:T(8,128)(2,1)S(1)} %copy-done.1, ...), custom_call_target="tpu_custom_call" | custom-call | tf_op jit(solution)/shard_map/pallas_call | solution.py:222
  27.0 24.2 %all_to_all.16.pieces = bf16[4,1568,128]{2,1,0:T(8,128)(2,1)S(1)} all-to-all(bf16[4,1568,128]{2,1,0:T(8,128)(2,1)S(1)} %shard_map.57), channel_id=1, replica_groups={{0,1,2,3},{4,5,6,7},{8,9,10,11},{12,13,14,15},{16,17,18,19},{20,21,22,2..., dimensions={0} | all-to-all | bytes 3211264 | tf_op jit(solution)/shard_map/all_to_all | solution.py:234
  51.2 1.0 %shard_map.58 = bf16[8,200,128]{2,1,0:T(8,128)(2,1)} custom-call(bf16[4,1568,128]{2,1,0:T(8,128)(2,1)S(1)} %all_to_all.16.pieces), custom_call_target="tpu_custom_call" | custom-call | tf_op jit(solution)/shard_map/pallas_call | solution.py:236
  52.1 14.9 %all-to-all-start.2 = ((bf16[8,200,128]{2,1,0:T(8,128)(2,1)}), bf16[8,200,128]{2,1,0:T(8,128)(2,1)S(1)}, u32[]{:S(2)}, u32[]{:S(2)}) async-start(bf16[8,200,128]{2,1,0:T(8,128)(2,1)} %shard_map.58), calls=%async_computation.2 | async-start | bytes 819200 | tf_op jit(solution)/shard_map/all_to_all | solution.py:243
  67.0 27.1 %all-to-all-done.2.pieces = bf16[8,200,128]{2,1,0:T(8,128)(2,1)S(1)} async-done(((bf16[8,200,128]{2,1,0:T(8,128)(2,1)}), bf16[8,200,128]{2,1,0:T(8,128)(2,1)S(1)}, u32[]{:S(2)}, u32[]{:S(2)}) %all-to-all-start.2) | async-done | bytes 409632 | tf_op jit(solution)/shard_map/all_to_all | solution.py:243
  94.1 0.9 shard_map.59
Async XLA Ops:
  0.7 22.0 %copy-start = (bf16[64,128,128]{2,1,0:T(8,128)(2,1)S(1)}, bf16[64,128,128]{2,1,0:T(8,128)(2,1)}, u32[]{:S(2)}) copy-start(bf16[64,128,128]{2,1,0:T(8,128)(2,1)} %values.3) | copy-start | bytes 6291460
  0.7 22.0 %copy-start.2 = (s32[64,2]{0,1:T(2,128)S(1)}, s32[64,2]{0,1:T(2,128)}, u32[]{:S(2)}) copy-start(s32[64,2]{0,1:T(2,128)} %param.8) | copy-start | bytes 1540
  3.4 21.0 %copy-start.1 = (bf16[128,128]{1,0:T(8,128)(2,1)S(1)}, bf16[128,128]{1,0:T(8,128)(2,1)}, u32[]{:S(2)}) copy-start(bf16[128,128]{1,0:T(8,128)(2,1)} %weight.1) | copy-start | bytes 98308
  20.7 3.7 %collective-permute-start = (bf16[8,240,128]{2,1,0:T(8,128)(2,1)S(1)}, bf16[8,240,128]{2,1,0:T(8,128)(2,1)S(1)}, u32[]{:S(2)}, u32[]{:S(2)}) collective-permute-start(bf16[8,240,128]{2,1,0:T(8,128)(2,1)S(1)} %all_to_all.15.mine), channel_id=1, source_target_pairs={{0,32},{32,0},{64,96},{96,64},{128,160},{160,128},{192,224},{224,1... | collective-permute-start | bytes 1474568 | tf_op jit(solution)/shard_map/ppermute | solution.py:210
  52.1 42.0 %all-to-all-start.2 = ((bf16[8,200,128]{2,1,0:T(8,128)(2,1)}), bf16[8,200,128]{2,1,0:T(8,128)(2,1)S(1)}, u32[]{:S(2)}, u32[]{:S(2)}) async-start(bf16[8,200,128]{2,1,0:T(8,128)(2,1)} %shard_map.58), calls=%async_computation.2 | async-start | bytes 819200 | tf_op jit(solution)/shard_map/all_to_all | solution.py:243

commit v4 on v3

--- a/solution.py
+++ b/solution.py
@@ -25,7 +25,18 @@
 FAR_ROWS = OWN + 8
 
 CHIP_GROUPS = [[2 * m + core for m in range(CHIPS)] for core in range(2)]
-NEAR_GROUPS = [[NEAR * far + near for near in range(NEAR)] for far in range(FAR)]
+
+
+def near_groups():
+    groups = []
+    for row in range(N_ROW):
+        for far in range(FAR):
+            even = (far + row % 2) % FAR
+            zs = (2 * even, 2 * far + 1)
+            groups.append([row * N_COL + 2 * zs[near // 2] + near % 2 for near in range(NEAR)])
+    return groups
+
+
 FAR_GROUPS = [[NEAR * far + near for far in range(FAR)] for near in range(NEAR)]
 
 VMEM = pl.BlockSpec(memory_space=pltpu.VMEM)
@@ -231,7 +242,7 @@
         ],
         compiler_params=params(),
     )(core, block_counts, coords, mine, other, weight, block_values, row_sums)
-    partial = lax.all_to_all(partial, "col", 0, 0, axis_index_groups=NEAR_GROUPS, tiled=True)
+    partial = lax.all_to_all(partial, ("row", "col"), 0, 0, axis_index_groups=near_groups(), tiled=True)
 
     reduced = pl.pallas_call(
         near_kernel,

time: 95.4 us -> 93.1 us (0.976)
  the two profiles are of different devices: /device:TPU:2 before, /device:TPU:24 now
where the time goes in v4:
time: 93.1 us; the launch traced here: 92.7 us
  blocking collectives  34.1 us (37%)
  waiting for transfers between devices  27.8 us (30%)
  starting transfers between devices  22.8 us (24%)
  Pallas kernels  7.24 us (8%)
    all_to_all x1, waiting for transfers between devices, shards(): lax.all_to_all(reduced, 'col', 0, 0, axis_index_groups=FAR_GROUPS, tiled=...  26.9 us
    all_to_all x1, starting transfers between devices, shards(): lax.all_to_all(reduced, 'col', 0, 0, axis_index_groups=FAR_GROUPS, tiled=...  20.9 us
    all_to_all x1, blocking collectives, shards(): lax.all_to_all(partial, ('row', 'col'), 0, 0, axis_index_groups=near_grou...  17.1 us
    all_to_all x1, blocking collectives, shards(): lax.all_to_all(outgoing, 'row', 0, 0, axis_index_groups=CHIP_GROUPS, tile...  17 us
    pallas_call x1, Pallas kernels, shards(): pl.pallas_call(column_sums_kernel, out_shape=jax.ShapeDtypeStruct((CHIPS,...  2.55 us
    ppermute x1, starting transfers between devices, shards(): other = lax.ppermute(mine, 'row', [(r, r ^ 1) for r in range(N_ROW)])  1.91 us
    pallas_call x1, Pallas kernels, shards(): pl.pallas_call(aggregate_kernel, out_shape=jax.ShapeDtypeStruct((NEAR, NE...  1.9 us
  transfers between devices with their start and end apart: 2, of which 2 were waited for; matrix products, arithmetic and copies ran while one was open for 0% of the time, Pallas kernels for 1%

profile of v4, /device:TPU:24, one launch (start us, length us, event | category | flops | bytes accessed | tf_op | source)
XLA Modules:
  0.0 92.7 jit_solution(6971509291084199583)
XLA Ops:
  0.7 0.0 copy-start
  0.7 0.0 copy-start.2
  0.7 2.5 %shard_map.55 = bf16[8,240,128]{2,1,0:T(8,128)(2,1)} custom-call(s32[1]{0:T(128)S(6)} %copy.6.counts_in.counts, s32[2,64]{1,0:T(2,128)} %bitcast.3, bf16[64,128,128]{2,1,0:T(8,128)(2,1)} %values.3, bf16[192,128]{1,0:T(8,128)(2,1)} %features_in.1), custom_call_target="tpu_custom_call" | custom-call | tf_op jit(solution)/shard_map/pallas_call | solution.py:203
  3.2 0.0 copy-start.1
  3.2 17.0 %all_to_all.15.mine = bf16[8,240,128]{2,1,0:T(8,128)(2,1)S(1)} all-to-all(bf16[8,240,128]{2,1,0:T(8,128)(2,1)} %shard_map.55), channel_id=1, replica_groups={{0,64,128,192,256,320,384,448},{32,96,160,224,288,352,416,480},{1,65,12..., dimensions={0} | all-to-all | bytes 983040 | tf_op jit(solution)/shard_map/all_to_all | solution.py:220
  20.2 1.9 %collective-permute-start = (bf16[8,240,128]{2,1,0:T(8,128)(2,1)S(1)}, bf16[8,240,128]{2,1,0:T(8,128)(2,1)S(1)}, u32[]{:S(2)}, u32[]{:S(2)}) collective-permute-start(bf16[8,240,128]{2,1,0:T(8,128)(2,1)S(1)} %all_to_all.15.mine), channel_id=1, source_target_pairs={{0,32},{32,0},{64,96},{96,64},{128,160},{160,128},{192,224},{224,1... | collective-permute-start | bytes 1474568 | tf_op jit(solution)/shard_map/ppermute | solution.py:221
  22.2 0.0 copy-done
  22.2 0.0 copy-done.2
  22.2 0.9 %shard_map.56.row_sums = bf16[4,32,128]{2,1,0:T(8,128)(2,1)S(1)} custom-call(bf16[8,240,128]{2,1,0:T(8,128)(2,1)S(1)} %all_to_all.15.mine, s32[1]{0:T(128)S(6)} %copy.6.counts_in.counts, s32[2,64]{1,0:T(2,128)S(1)} %bitcast.4, bf16[64,128,128]{2,1,0:T(8,128)(2,1)S(1)} %copy-done), custom_call_target="tpu_custom_call" | custom-call | flops 268435456 | bytes 2097152 | tf_op jit(solution)/shard_map/pallas_call | solution.py:223
  23.2 0.8 collective-permute-done.other
  24.0 0.0 copy-done.1
  24.0 1.9 %shard_map.57 = bf16[4,1568,128]{2,1,0:T(8,128)(2,1)S(1)} custom-call(s32[1]{0:T(128)} %bitcast.1.core, s32[1]{0:T(128)S(6)} %copy.6.counts_in.counts, s32[2,64]{1,0:T(2,128)S(1)} %bitcast.5, bf16[8,240,128]{2,1,0:T(8,128)(2,1)S(1)} %all_to_all.15.mine, bf16[8,240,128]{2,1,0:T(8,128)(2,1)S(1)} %collective-permute-done.other, bf16[128,128]{1,0:T(8,128)(2,1)S(1)} %copy-done.1, ...), custom_call_target="tpu_custom_call" | custom-call | tf_op jit(solution)/shard_map/pallas_call | solution.py:233
  25.9 17.1 %all_to_all.16.pieces = bf16[4,1568,128]{2,1,0:T(8,128)(2,1)S(1)} all-to-all(bf16[4,1568,128]{2,1,0:T(8,128)(2,1)S(1)} %shard_map.57), channel_id=1, replica_groups={{0,1,2,3},{4,5,6,7},{8,9,10,11},{12,13,14,15},{16,17,18,19},{20,21,22,2..., dimensions={0} | all-to-all | bytes 3211264 | tf_op jit(solution)/shard_map/all_to_all | solution.py:245
  43.0 1.0 %shard_map.58 = bf16[8,200,128]{2,1,0:T(8,128)(2,1)} custom-call(bf16[4,1568,128]{2,1,0:T(8,128)(2,1)S(1)} %all_to_all.16.pieces), custom_call_target="tpu_custom_call" | custom-call | tf_op jit(solution)/shard_map/pallas_call | solution.py:247
  44.0 20.9 %all-to-all-start.2 = ((bf16[8,200,128]{2,1,0:T(8,128)(2,1)}), bf16[8,200,128]{2,1,0:T(8,128)(2,1)S(1)}, u32[]{:S(2)}, u32[]{:S(2)}) async-start(bf16[8,200,128]{2,1,0:T(8,128)(2,1)} %shard_map.58), calls=%async_computation.2 | async-start | bytes 819200 | tf_op jit(solution)/shard_map/all_to_all | solution.py:254
  64.8 26.9 %all-to-all-done.2.pieces = bf16[8,200,128]{2,1,0:T(8,128)(2,1)S(1)} async-done(((bf16[8,200,128]{2,1,0:T(8,128)(2,1)}), bf16[8,200,128]{2,1,0:T(8,128)(2,1)S(1)}, u32[]{:S(2)}, u32[]{:S(2)}) %all-to-all-start.2) | async-done | bytes 409632 | tf_op jit(solution)/shard_map/all_to_all | solution.py:254
  91.8 0.9 shard_map.59
Async XLA Ops:
  0.7 21.5 %copy-start = (bf16[64,128,128]{2,1,0:T(8,128)(2,1)S(1)}, bf16[64,128,128]{2,1,0:T(8,128)(2,1)}, u32[]{:S(2)}) copy-start(bf16[64,128,128]{2,1,0:T(8,128)(2,1)} %values.3) | copy-start | bytes 6291460
  0.7 21.5 %copy-start.2 = (s32[64,2]{0,1:T(2,128)S(1)}, s32[64,2]{0,1:T(2,128)}, u32[]{:S(2)}) copy-start(s32[64,2]{0,1:T(2,128)} %param.8) | copy-start | bytes 1540
  3.2 20.8 %copy-start.1 = (bf16[128,128]{1,0:T(8,128)(2,1)S(1)}, bf16[128,128]{1,0:T(8,128)(2,1)}, u32[]{:S(2)}) copy-start(bf16[128,128]{1,0:T(8,128)(2,1)} %weight.1) | copy-start | bytes 98308
  20.2 3.7 %collective-permute-start = (bf16[8,240,128]{2,1,0:T(8,128)(2,1)S(1)}, bf16[8,240,128]{2,1,0:T(8,128)(2,1)S(1)}, u32[]{:S(2)}, u32[]{:S(2)}) collective-permute-start(bf16[8,240,128]{2,1,0:T(8,128)(2,1)S(1)} %all_to_all.15.mine), channel_id=1, source_target_pairs={{0,32},{32,0},{64,96},{96,64},{128,160},{160,128},{192,224},{224,1... | collective-permute-start | bytes 1474568 | tf_op jit(solution)/shard_map/ppermute | solution.py:221
  44.0 47.8 %all-to-all-start.2 = ((bf16[8,200,128]{2,1,0:T(8,128)(2,1)}), bf16[8,200,128]{2,1,0:T(8,128)(2,1)S(1)}, u32[]{:S(2)}, u32[]{:S(2)}) async-start(bf16[8,200,128]{2,1,0:T(8,128)(2,1)} %shard_map.58), calls=%async_computation.2 | async-start | bytes 819200 | tf_op jit(solution)/shard_map/all_to_all | solution.py:254

commit v5 on v4

--- a/solution.py
+++ b/solution.py
@@ -18,9 +18,9 @@
 FAR = N_COL // NEAR
 HALF = 64
 UNROLL = 8
-BATCH = 16
-
-GATHER_ROWS = OWN + 2 * COL_BLOCKS
+BATCH = 32
+
+GATHER_ROWS = OWN + COL_BLOCKS
 NEAR_ROWS = FAR * OWN + 4 * FAR
 FAR_ROWS = OWN + 8
 
@@ -51,7 +51,7 @@
     return high, value - high
 
 
-def column_sums_kernel(counts_in, coords_in, values_in, features_in, out, counts, coords, values, features, sums, parts, small_sems, sems):
+def column_sums_kernel(counts_in, coords_in, values_in, features_in, out, counts, coords, values, features, sums, small_sems, sems):
     small = [
         pltpu.make_async_copy(counts_in, counts, small_sems.at[0]),
         pltpu.make_async_copy(coords_in, coords, small_sems.at[1]),
@@ -81,11 +81,8 @@
                 col = jnp.where(slot < live, coords[1, slot], COL_BLOCKS)
                 sums[pl.ds(col, 1), :] += jnp.sum(values[slot].astype(f32), axis=0, keepdims=True)
 
-    high, low = split(sums[:COL_BLOCKS])
-    parts[:COL_BLOCKS] = high
-    parts[COL_BLOCKS:] = low
     for m in range(CHIPS):
-        out[m, OWN:] = parts[...].astype(bf16)
+        out[m, OWN:] = sums[:COL_BLOCKS].astype(bf16)
 
 
 def row_sums_kernel(mine, counts, coords, values, out, sums):
@@ -115,10 +112,10 @@
 
 def aggregate_kernel(core, counts, coords, mine, other, weight, values, row_sums, out, scales, scaled, total):
     live = counts[0]
-    sums = jnp.zeros((2 * COL_BLOCKS, BLK), f32)
+    sums = jnp.zeros((COL_BLOCKS, BLK), f32)
     for m in range(CHIPS):
         sums += mine[m, OWN:].astype(f32) + other[m, OWN:].astype(f32)
-    degree = 1.0 + (sums[:COL_BLOCKS] + sums[COL_BLOCKS:])
+    degree = 1.0 + sums
     scales[...] = jnp.zeros_like(scales)
     scales[:COL_BLOCKS] = lax.rsqrt(degree)
     scales[...] = scales[...].T
@@ -211,7 +208,6 @@
             pltpu.VMEM((SLOTS, BLK, BLK), bf16),
             pltpu.VMEM((OWN, F), bf16),
             pltpu.VMEM((32, BLK), f32),
-            pltpu.VMEM((2 * COL_BLOCKS, BLK), f32),
             pltpu.SemaphoreType.DMA((3,)),
             pltpu.SemaphoreType.DMA((SLOTS // UNROLL,)),
         ],

time: 93.1 us -> 91.1 us (0.979)
  the two profiles are of different devices: /device:TPU:24 before, /device:TPU:42 now
where the time goes in v5:
time: 91.1 us; the launch traced here: 90.7 us
  blocking collectives  38.2 us (42%)
  waiting for transfers between devices  26.9 us (30%)
  starting transfers between devices  16.1 us (18%)
  Pallas kernels  8.73 us (10%)
    all_to_all x1, waiting for transfers between devices, shards(): lax.all_to_all(reduced, 'col', 0, 0, axis_index_groups=FAR_GROUPS, tiled=...  26.7 us
    all_to_all x1, blocking collectives, shards(): lax.all_to_all(partial, ('row', 'col'), 0, 0, axis_index_groups=near_grou...  22.9 us
    all_to_all x1, blocking collectives, shards(): lax.all_to_all(outgoing, 'row', 0, 0, axis_index_groups=CHIP_GROUPS, tile...  15.3 us
    all_to_all x1, starting transfers between devices, shards(): lax.all_to_all(reduced, 'col', 0, 0, axis_index_groups=FAR_GROUPS, tiled=...  14.2 us
    pallas_call x1, Pallas kernels, shards(): pl.pallas_call(column_sums_kernel, out_shape=jax.ShapeDtypeStruct((CHIPS,...  2.85 us
    pallas_call x1, Pallas kernels, shards(): pl.pallas_call(aggregate_kernel, out_shape=jax.ShapeDtypeStruct((NEAR, NE...  2.53 us
    ppermute x1, starting transfers between devices, shards(): other = lax.ppermute(mine, 'row', [(r, r ^ 1) for r in range(N_ROW)])  1.91 us
  transfers between devices with their start and end apart: 2, of which 2 were waited for; matrix products, arithmetic and copies ran while one was open for 0% of the time, Pallas kernels for 2%

profile of v5, /device:TPU:42, one launch (start us, length us, event | category | flops | bytes accessed | tf_op | source)
XLA Modules:
  0.0 90.7 jit_solution(27567270787132335)
XLA Ops:
  0.7 0.0 copy-start
  0.7 0.0 copy-start.2
  0.7 2.8 %shard_map.55 = bf16[8,216,128]{2,1,0:T(8,128)(2,1)} custom-call(s32[1]{0:T(128)S(6)} %copy.6.counts_in.counts, s32[2,64]{1,0:T(2,128)} %bitcast.3, bf16[64,128,128]{2,1,0:T(8,128)(2,1)} %values.3, bf16[192,128]{1,0:T(8,128)(2,1)} %features_in.1), custom_call_target="tpu_custom_call" | custom-call | tf_op jit(solution)/shard_map/pallas_call | solution.py:200
  3.5 0.0 copy-start.1
  3.5 15.3 %all_to_all.15.mine = bf16[8,216,128]{2,1,0:T(8,128)(2,1)S(1)} all-to-all(bf16[8,216,128]{2,1,0:T(8,128)(2,1)} %shard_map.55), channel_id=1, replica_groups={{0,64,128,192,256,320,384,448},{32,96,160,224,288,352,416,480},{1,65,12..., dimensions={0} | all-to-all | bytes 884736 | tf_op jit(solution)/shard_map/all_to_all | solution.py:216
  18.9 1.9 %collective-permute-start = (bf16[8,216,128]{2,1,0:T(8,128)(2,1)S(1)}, bf16[8,216,128]{2,1,0:T(8,128)(2,1)S(1)}, u32[]{:S(2)}, u32[]{:S(2)}) collective-permute-start(bf16[8,216,128]{2,1,0:T(8,128)(2,1)S(1)} %all_to_all.15.mine), channel_id=1, source_target_pairs={{0,32},{32,0},{64,96},{96,64},{128,160},{160,128},{192,224},{224,1... | collective-permute-start | bytes 1327112 | tf_op jit(solution)/shard_map/ppermute | solution.py:217
  20.8 0.0 copy-done
  20.8 0.0 copy-done.2
  20.8 1.5 %shard_map.56.row_sums = bf16[4,32,128]{2,1,0:T(8,128)(2,1)S(1)} custom-call(bf16[8,216,128]{2,1,0:T(8,128)(2,1)S(1)} %all_to_all.15.mine, s32[1]{0:T(128)S(6)} %copy.6.counts_in.counts, s32[2,64]{1,0:T(2,128)S(1)} %bitcast.4, bf16[64,128,128]{2,1,0:T(8,128)(2,1)S(1)} %copy-done), custom_call_target="tpu_custom_call" | custom-call | flops 268435456 | bytes 2097152 | tf_op jit(solution)/shard_map/pallas_call | solution.py:219
  22.3 0.2 collective-permute-done.other
  22.5 0.0 copy-done.1
  22.5 2.5 %shard_map.57 = bf16[4,1568,128]{2,1,0:T(8,128)(2,1)S(1)} custom-call(s32[1]{0:T(128)} %bitcast.1.core, s32[1]{0:T(128)S(6)} %copy.6.counts_in.counts, s32[2,64]{1,0:T(2,128)S(1)} %bitcast.5, bf16[8,216,128]{2,1,0:T(8,128)(2,1)S(1)} %all_to_all.15.mine, bf16[8,216,128]{2,1,0:T(8,128)(2,1)S(1)} %collective-permute-done.other, bf16[128,128]{1,0:T(8,128)(2,1)S(1)} %copy-done.1, ...), custom_call_target="tpu_custom_call" | custom-call | tf_op jit(solution)/shard_map/pallas_call | solution.py:229
  25.1 22.9 %all_to_all.16.pieces = bf16[4,1568,128]{2,1,0:T(8,128)(2,1)S(1)} all-to-all(bf16[4,1568,128]{2,1,0:T(8,128)(2,1)S(1)} %shard_map.57), channel_id=1, replica_groups={{0,1,2,3},{4,5,6,7},{8,9,10,11},{12,13,14,15},{16,17,18,19},{20,21,22,2..., dimensions={0} | all-to-all | bytes 3211264 | tf_op jit(solution)/shard_map/all_to_all | solution.py:241
  48.0 1.0 %shard_map.58 = bf16[8,200,128]{2,1,0:T(8,128)(2,1)} custom-call(bf16[4,1568,128]{2,1,0:T(8,128)(2,1)S(1)} %all_to_all.16.pieces), custom_call_target="tpu_custom_call" | custom-call | tf_op jit(solution)/shard_map/pallas_call | solution.py:243
  49.0 14.2 %all-to-all-start.2 = ((bf16[8,200,128]{2,1,0:T(8,128)(2,1)}), bf16[8,200,128]{2,1,0:T(8,128)(2,1)S(1)}, u32[]{:S(2)}, u32[]{:S(2)}) async-start(bf16[8,200,128]{2,1,0:T(8,128)(2,1)} %shard_map.58), calls=%async_computation.2 | async-start | bytes 819200 | tf_op jit(solution)/shard_map/all_to_all | solution.py:250
  63.1 26.7 %all-to-all-done.2.pieces = bf16[8,200,128]{2,1,0:T(8,128)(2,1)S(1)} async-done(((bf16[8,200,128]{2,1,0:T(8,128)(2,1)}), bf16[8,200,128]{2,1,0:T(8,128)(2,1)S(1)}, u32[]{:S(2)}, u32[]{:S(2)}) %all-to-all-start.2) | async-done | bytes 409632 | tf_op jit(solution)/shard_map/all_to_all | solution.py:250
  89.8 0.9 shard_map.59
Async XLA Ops:
  0.7 20.1 %copy-start = (bf16[64,128,128]{2,1,0:T(8,128)(2,1)S(1)}, bf16[64,128,128]{2,1,0:T(8,128)(2,1)}, u32[]{:S(2)}) copy-start(bf16[64,128,128]{2,1,0:T(8,128)(2,1)} %values.3) | copy-start | bytes 6291460
  0.7 20.1 %copy-start.2 = (s32[64,2]{0,1:T(2,128)S(1)}, s32[64,2]{0,1:T(2,128)}, u32[]{:S(2)}) copy-start(s32[64,2]{0,1:T(2,128)} %param.8) | copy-start | bytes 1540
  3.5 19.0 %copy-start.1 = (bf16[128,128]{1,0:T(8,128)(2,1)S(1)}, bf16[128,128]{1,0:T(8,128)(2,1)}, u32[]{:S(2)}) copy-start(bf16[128,128]{1,0:T(8,128)(2,1)} %weight.1) | copy-start | bytes 98308
  18.9 3.7 %collective-permute-start = (bf16[8,216,128]{2,1,0:T(8,128)(2,1)S(1)}, bf16[8,216,128]{2,1,0:T(8,128)(2,1)S(1)}, u32[]{:S(2)}, u32[]{:S(2)}) collective-permute-start(bf16[8,216,128]{2,1,0:T(8,128)(2,1)S(1)} %all_to_all.15.mine), channel_id=1, source_target_pairs={{0,32},{32,0},{64,96},{96,64},{128,160},{160,128},{192,224},{224,1... | collective-permute-start | bytes 1327112 | tf_op jit(solution)/shard_map/ppermute | solution.py:217
  49.0 40.8 %all-to-all-start.2 = ((bf16[8,200,128]{2,1,0:T(8,128)(2,1)}), bf16[8,200,128]{2,1,0:T(8,128)(2,1)S(1)}, u32[]{:S(2)}, u32[]{:S(2)}) async-start(bf16[8,200,128]{2,1,0:T(8,128)(2,1)} %shard_map.58), calls=%async_computation.2 | async-start | bytes 819200 | tf_op jit(solution)/shard_map/all_to_all | solution.py:250

commit v6 on v5

--- a/solution.py
+++ b/solution.py
@@ -24,7 +24,15 @@
 NEAR_ROWS = FAR * OWN + 4 * FAR
 FAR_ROWS = OWN + 8
 
-CHIP_GROUPS = [[2 * m + core for m in range(CHIPS)] for core in range(2)]
+CHIP_TURN = 5
+FAR_TURN = 4
+
+
+def owner(near, far):
+    return NEAR * ((far + FAR_TURN) % FAR) + near
+
+
+CHIP_GROUPS = [[2 * ((m + CHIP_TURN) % CHIPS) + core for m in range(CHIPS)] for core in range(2)]
 
 
 def near_groups():
@@ -37,7 +45,7 @@
     return groups
 
 
-FAR_GROUPS = [[NEAR * far + near for far in range(FAR)] for near in range(NEAR)]
+FAR_GROUPS = [[owner(near, far) for far in range(FAR)] for near in range(NEAR)]
 
 VMEM = pl.BlockSpec(memory_space=pltpu.VMEM)
 SMEM = pl.BlockSpec(memory_space=pltpu.SMEM)
@@ -105,7 +113,7 @@
         picks = []
         for part in (high, low):
             for far in range(FAR):
-                first = (far * NEAR + near) * OWN // BLK
+                first = owner(near, far) * OWN // BLK
                 picks.append(part[first : first + 2])
         out[near] = jnp.concatenate(picks, axis=0).astype(bf16)
 
@@ -122,7 +130,7 @@
 
     def scale(pieces):
         for r in range(N_ROW):
-            transformed = jnp.dot(pieces[r % 2][r // 2, :OWN], weight[...], preferred_element_type=f32)
+            transformed = jnp.dot(pieces[r % 2][(r // 2 - CHIP_TURN) % CHIPS, :OWN], weight[...], preferred_element_type=f32)
             for part in range(OWN // HALF):
                 h = r * (OWN // HALF) + part
                 factor = scales[(h % 2) * HALF : (h % 2 + 1) * HALF, h // 2 : h // 2 + 1]
@@ -155,7 +163,7 @@
 
     for near in range(NEAR):
         for far in range(FAR):
-            dest = far * NEAR + near
+            dest = owner(near, far)
             out[near, far * OWN : (far + 1) * OWN] = total[dest * OWN : (dest + 1) * OWN].astype(bf16)
         out[near, FAR * OWN :] = row_sums[near]
 

time: 91.1 us -> 86.2 us (0.946)
  the two profiles are of different devices: /device:TPU:42 before, /device:TPU:32 now
where the time goes in v6:
time: 86.2 us; the launch traced here: 85.8 us
  blocking collectives  39 us (45%)
  starting transfers between devices  19.2 us (22%)
  waiting for transfers between devices  18.2 us (21%)
  Pallas kernels  8.62 us (10%)
    all_to_all x1, blocking collectives, shards(): lax.all_to_all(partial, ('row', 'col'), 0, 0, axis_index_groups=near_grou...  24 us
    all_to_all x1, waiting for transfers between devices, shards(): lax.all_to_all(reduced, 'col', 0, 0, axis_index_groups=FAR_GROUPS, tiled=...  18 us
    all_to_all x1, starting transfers between devices, shards(): lax.all_to_all(reduced, 'col', 0, 0, axis_index_groups=FAR_GROUPS, tiled=...  17.3 us
    all_to_all x1, blocking collectives, shards(): lax.all_to_all(outgoing, 'row', 0, 0, axis_index_groups=CHIP_GROUPS, tile...  15 us
    pallas_call x1, Pallas kernels, shards(): pl.pallas_call(column_sums_kernel, out_shape=jax.ShapeDtypeStruct((CHIPS,...  2.74 us
    pallas_call x1, Pallas kernels, shards(): pl.pallas_call(aggregate_kernel, out_shape=jax.ShapeDtypeStruct((NEAR, NE...  2.53 us
    ppermute x1, starting transfers between devices, shards(): other = lax.ppermute(mine, 'row', [(r, r ^ 1) for r in range(N_ROW)])  1.91 us
  transfers between devices with their start and end apart: 2, of which 2 were waited for; matrix products, arithmetic and copies ran while one was open for 0% of the time, Pallas kernels for 2%

profile of v6, /device:TPU:32, one launch (start us, length us, event | category | flops | bytes accessed | tf_op | source)
XLA Modules:
  0.0 85.8 jit_solution(14357750976418752814)
XLA Ops:
  0.7 0.0 copy-start
  0.7 0.0 copy-start.2
  0.7 2.7 %shard_map.55 = bf16[8,216,128]{2,1,0:T(8,128)(2,1)} custom-call(s32[1]{0:T(128)S(6)} %copy.6.counts_in.counts, s32[2,64]{1,0:T(2,128)} %bitcast.3, bf16[64,128,128]{2,1,0:T(8,128)(2,1)} %values.3, bf16[192,128]{1,0:T(8,128)(2,1)} %features_in.1), custom_call_target="tpu_custom_call" | custom-call | tf_op jit(solution)/shard_map/pallas_call | solution.py:208
  3.4 0.0 copy-start.1
  3.4 15.0 %all_to_all.15.mine = bf16[8,216,128]{2,1,0:T(8,128)(2,1)S(1)} all-to-all(bf16[8,216,128]{2,1,0:T(8,128)(2,1)} %shard_map.55), channel_id=1, replica_groups={{320,384,448,0,64,128,192,256},{352,416,480,32,96,160,224,288},{321,385..., dimensions={0} | all-to-all | bytes 884736 | tf_op jit(solution)/shard_map/all_to_all | solution.py:224
  18.4 1.9 %collective-permute-start = (bf16[8,216,128]{2,1,0:T(8,128)(2,1)S(1)}, bf16[8,216,128]{2,1,0:T(8,128)(2,1)S(1)}, u32[]{:S(2)}, u32[]{:S(2)}) collective-permute-start(bf16[8,216,128]{2,1,0:T(8,128)(2,1)S(1)} %all_to_all.15.mine), channel_id=1, source_target_pairs={{0,32},{32,0},{64,96},{96,64},{128,160},{160,128},{192,224},{224,1... | collective-permute-start | bytes 1327112 | tf_op jit(solution)/shard_map/ppermute | solution.py:225
  20.4 0.0 copy-done
  20.4 0.0 copy-done.2
  20.4 1.5 %shard_map.56.row_sums = bf16[4,32,128]{2,1,0:T(8,128)(2,1)S(1)} custom-call(bf16[8,216,128]{2,1,0:T(8,128)(2,1)S(1)} %all_to_all.15.mine, s32[1]{0:T(128)S(6)} %copy.6.counts_in.counts, s32[2,64]{1,0:T(2,128)S(1)} %bitcast.4, bf16[64,128,128]{2,1,0:T(8,128)(2,1)S(1)} %copy-done), custom_call_target="tpu_custom_call" | custom-call | flops 268435456 | bytes 2097152 | tf_op jit(solution)/shard_map/pallas_call | solution.py:227
  21.9 0.2 collective-permute-done.other
  22.1 0.0 copy-done.1
  22.1 2.5 %shard_map.57 = bf16[4,1568,128]{2,1,0:T(8,128)(2,1)S(1)} custom-call(s32[1]{0:T(128)} %bitcast.1.core, s32[1]{0:T(128)S(6)} %copy.6.counts_in.counts, s32[2,64]{1,0:T(2,128)S(1)} %bitcast.5, bf16[8,216,128]{2,1,0:T(8,128)(2,1)S(1)} %all_to_all.15.mine, bf16[8,216,128]{2,1,0:T(8,128)(2,1)S(1)} %collective-permute-done.other, bf16[128,128]{1,0:T(8,128)(2,1)S(1)} %copy-done.1, ...), custom_call_target="tpu_custom_call" | custom-call | tf_op jit(solution)/shard_map/pallas_call | solution.py:237
  24.7 24.0 %all_to_all.16.pieces = bf16[4,1568,128]{2,1,0:T(8,128)(2,1)S(1)} all-to-all(bf16[4,1568,128]{2,1,0:T(8,128)(2,1)S(1)} %shard_map.57), channel_id=1, replica_groups={{0,1,2,3},{4,5,6,7},{8,9,10,11},{12,13,14,15},{16,17,18,19},{20,21,22,2..., dimensions={0} | all-to-all | bytes 3211264 | tf_op jit(solution)/shard_map/all_to_all | solution.py:249
  48.7 1.0 %shard_map.58 = bf16[8,200,128]{2,1,0:T(8,128)(2,1)} custom-call(bf16[4,1568,128]{2,1,0:T(8,128)(2,1)S(1)} %all_to_all.16.pieces), custom_call_target="tpu_custom_call" | custom-call | tf_op jit(solution)/shard_map/pallas_call | solution.py:251
  49.7 17.3 %all-to-all-start.2 = ((bf16[8,200,128]{2,1,0:T(8,128)(2,1)}), bf16[8,200,128]{2,1,0:T(8,128)(2,1)S(1)}, u32[]{:S(2)}, u32[]{:S(2)}) async-start(bf16[8,200,128]{2,1,0:T(8,128)(2,1)} %shard_map.58), calls=%async_computation.2 | async-start | bytes 819200 | tf_op jit(solution)/shard_map/all_to_all | solution.py:258
  66.9 18.0 %all-to-all-done.2.pieces = bf16[8,200,128]{2,1,0:T(8,128)(2,1)S(1)} async-done(((bf16[8,200,128]{2,1,0:T(8,128)(2,1)}), bf16[8,200,128]{2,1,0:T(8,128)(2,1)S(1)}, u32[]{:S(2)}, u32[]{:S(2)}) %all-to-all-start.2) | async-done | bytes 409632 | tf_op jit(solution)/shard_map/all_to_all | solution.py:258
  84.9 0.9 %shard_map.59 = bf16[192,128]{1,0:T(8,128)(2,1)} custom-call(s32[1]{0:T(128)} %bitcast.odd, bf16[8,200,128]{2,1,0:T(8,128)(2,1)S(1)} %all-to-all-done.2.pieces), custom_call_target="tpu_custom_call" | custom-call | tf_op jit(solution)/shard_map/pallas_call | solution.py:260
Async XLA Ops:
  0.7 19.7 %copy-start = (bf16[64,128,128]{2,1,0:T(8,128)(2,1)S(1)}, bf16[64,128,128]{2,1,0:T(8,128)(2,1)}, u32[]{:S(2)}) copy-start(bf16[64,128,128]{2,1,0:T(8,128)(2,1)} %values.3) | copy-start | bytes 6291460
  0.7 19.7 %copy-start.2 = (s32[64,2]{0,1:T(2,128)S(1)}, s32[64,2]{0,1:T(2,128)}, u32[]{:S(2)}) copy-start(s32[64,2]{0,1:T(2,128)} %param.8) | copy-start | bytes 1540
  3.4 18.7 %copy-start.1 = (bf16[128,128]{1,0:T(8,128)(2,1)S(1)}, bf16[128,128]{1,0:T(8,128)(2,1)}, u32[]{:S(2)}) copy-start(bf16[128,128]{1,0:T(8,128)(2,1)} %weight.1) | copy-start | bytes 98308
  18.4 3.7 %collective-permute-start = (bf16[8,216,128]{2,1,0:T(8,128)(2,1)S(1)}, bf16[8,216,128]{2,1,0:T(8,128)(2,1)S(1)}, u32[]{:S(2)}, u32[]{:S(2)}) collective-permute-start(bf16[8,216,128]{2,1,0:T(8,128)(2,1)S(1)} %all_to_all.15.mine), channel_id=1, source_target_pairs={{0,32},{32,0},{64,96},{96,64},{128,160},{160,128},{192,224},{224,1... | collective-permute-start | bytes 1327112 | tf_op jit(solution)/shard_map/ppermute | solution.py:225
  49.7 35.3 %all-to-all-start.2 = ((bf16[8,200,128]{2,1,0:T(8,128)(2,1)}), bf16[8,200,128]{2,1,0:T(8,128)(2,1)S(1)}, u32[]{:S(2)}, u32[]{:S(2)}) async-start(bf16[8,200,128]{2,1,0:T(8,128)(2,1)} %shard_map.58), calls=%async_computation.2 | async-start | bytes 819200 | tf_op jit(solution)/shard_map/all_to_all | solution.py:258

commit v7 on v6

--- a/solution.py
+++ b/solution.py
@@ -24,8 +24,8 @@
 NEAR_ROWS = FAR * OWN + 4 * FAR
 FAR_ROWS = OWN + 8
 
-CHIP_TURN = 5
-FAR_TURN = 4
+CHIP_TURN = 7
+FAR_TURN = 5
 
 
 def owner(near, far):

time: 86.2 us -> 84.7 us (0.983)
  the two profiles are of different devices: /device:TPU:32 before, /device:TPU:28 now
where the time goes in v7:
time: 84.7 us; the launch traced here: 84.3 us
  blocking collectives  33.8 us (40%)
  starting transfers between devices  21.5 us (25%)
  waiting for transfers between devices  19.4 us (23%)
  Pallas kernels  8.79 us (10%)
    all_to_all x1, starting transfers between devices, shards(): lax.all_to_all(reduced, 'col', 0, 0, axis_index_groups=FAR_GROUPS, tiled=...  19.6 us
    all_to_all x1, waiting for transfers between devices, shards(): lax.all_to_all(reduced, 'col', 0, 0, axis_index_groups=FAR_GROUPS, tiled=...  19.2 us
    all_to_all x1, blocking collectives, shards(): lax.all_to_all(partial, ('row', 'col'), 0, 0, axis_index_groups=near_grou...  17.4 us
    all_to_all x1, blocking collectives, shards(): lax.all_to_all(outgoing, 'row', 0, 0, axis_index_groups=CHIP_GROUPS, tile...  16.4 us
    pallas_call x1, Pallas kernels, shards(): pl.pallas_call(column_sums_kernel, out_shape=jax.ShapeDtypeStruct((CHIPS,...  2.91 us
    pallas_call x1, Pallas kernels, shards(): pl.pallas_call(aggregate_kernel, out_shape=jax.ShapeDtypeStruct((NEAR, NE...  2.53 us
    ppermute x1, starting transfers between devices, shards(): other = lax.ppermute(mine, 'row', [(r, r ^ 1) for r in range(N_ROW)])  1.91 us
  transfers between devices with their start and end apart: 2, of which 2 were waited for; matrix products, arithmetic and copies ran while one was open for 0% of the time, Pallas kernels for 2%

profile of v7, /device:TPU:28, one launch (start us, length us, event | category | flops | bytes accessed | tf_op | source)
XLA Modules:
  0.0 84.3 jit_solution(7615595175246784977)
XLA Ops:
  0.7 0.0 copy-start
  0.7 0.0 copy-start.2
  0.7 2.9 %shard_map.55 = bf16[8,216,128]{2,1,0:T(8,128)(2,1)} custom-call(s32[1]{0:T(128)S(6)} %copy.6.counts_in.counts, s32[2,64]{1,0:T(2,128)} %bitcast.3, bf16[64,128,128]{2,1,0:T(8,128)(2,1)} %values.3, bf16[192,128]{1,0:T(8,128)(2,1)} %features_in.1), custom_call_target="tpu_custom_call" | custom-call | tf_op jit(solution)/shard_map/pallas_call | solution.py:208
  3.6 0.0 copy-start.1
  3.6 16.4 %all_to_all.15.mine = bf16[8,216,128]{2,1,0:T(8,128)(2,1)S(1)} all-to-all(bf16[8,216,128]{2,1,0:T(8,128)(2,1)} %shard_map.55), channel_id=1, replica_groups={{448,0,64,128,192,256,320,384},{480,32,96,160,224,288,352,416},{449,1,6..., dimensions={0} | all-to-all | bytes 884736 | tf_op jit(solution)/shard_map/all_to_all | solution.py:224
  20.0 1.9 %collective-permute-start = (bf16[8,216,128]{2,1,0:T(8,128)(2,1)S(1)}, bf16[8,216,128]{2,1,0:T(8,128)(2,1)S(1)}, u32[]{:S(2)}, u32[]{:S(2)}) collective-permute-start(bf16[8,216,128]{2,1,0:T(8,128)(2,1)S(1)} %all_to_all.15.mine), channel_id=1, source_target_pairs={{0,32},{32,0},{64,96},{96,64},{128,160},{160,128},{192,224},{224,1... | collective-permute-start | bytes 1327112 | tf_op jit(solution)/shard_map/ppermute | solution.py:225
  21.9 0.0 copy-done
  21.9 0.0 copy-done.2
  22.0 1.5 %shard_map.56.row_sums = bf16[4,32,128]{2,1,0:T(8,128)(2,1)S(1)} custom-call(bf16[8,216,128]{2,1,0:T(8,128)(2,1)S(1)} %all_to_all.15.mine, s32[1]{0:T(128)S(6)} %copy.6.counts_in.counts, s32[2,64]{1,0:T(2,128)S(1)} %bitcast.4, bf16[64,128,128]{2,1,0:T(8,128)(2,1)S(1)} %copy-done), custom_call_target="tpu_custom_call" | custom-call | flops 268435456 | bytes 2097152 | tf_op jit(solution)/shard_map/pallas_call | solution.py:227
  23.5 0.2 collective-permute-done.other
  23.7 0.0 copy-done.1
  23.7 2.5 %shard_map.57 = bf16[4,1568,128]{2,1,0:T(8,128)(2,1)S(1)} custom-call(s32[1]{0:T(128)} %bitcast.1.core, s32[1]{0:T(128)S(6)} %copy.6.counts_in.counts, s32[2,64]{1,0:T(2,128)S(1)} %bitcast.5, bf16[8,216,128]{2,1,0:T(8,128)(2,1)S(1)} %all_to_all.15.mine, bf16[8,216,128]{2,1,0:T(8,128)(2,1)S(1)} %collective-permute-done.other, bf16[128,128]{1,0:T(8,128)(2,1)S(1)} %copy-done.1, ...), custom_call_target="tpu_custom_call" | custom-call | tf_op jit(solution)/shard_map/pallas_call | solution.py:237
  26.2 17.4 %all_to_all.16.pieces = bf16[4,1568,128]{2,1,0:T(8,128)(2,1)S(1)} all-to-all(bf16[4,1568,128]{2,1,0:T(8,128)(2,1)S(1)} %shard_map.57), channel_id=1, replica_groups={{0,1,2,3},{4,5,6,7},{8,9,10,11},{12,13,14,15},{16,17,18,19},{20,21,22,2..., dimensions={0} | all-to-all | bytes 3211264 | tf_op jit(solution)/shard_map/all_to_all | solution.py:249
  43.6 1.0 %shard_map.58 = bf16[8,200,128]{2,1,0:T(8,128)(2,1)} custom-call(bf16[4,1568,128]{2,1,0:T(8,128)(2,1)S(1)} %all_to_all.16.pieces), custom_call_target="tpu_custom_call" | custom-call | tf_op jit(solution)/shard_map/pallas_call | solution.py:251
  44.6 19.6 %all-to-all-start.2 = ((bf16[8,200,128]{2,1,0:T(8,128)(2,1)}), bf16[8,200,128]{2,1,0:T(8,128)(2,1)S(1)}, u32[]{:S(2)}, u32[]{:S(2)}) async-start(bf16[8,200,128]{2,1,0:T(8,128)(2,1)} %shard_map.58), calls=%async_computation.2 | async-start | bytes 819200 | tf_op jit(solution)/shard_map/all_to_all | solution.py:258
  64.2 19.2 %all-to-all-done.2.pieces = bf16[8,200,128]{2,1,0:T(8,128)(2,1)S(1)} async-done(((bf16[8,200,128]{2,1,0:T(8,128)(2,1)}), bf16[8,200,128]{2,1,0:T(8,128)(2,1)S(1)}, u32[]{:S(2)}, u32[]{:S(2)}) %all-to-all-start.2) | async-done | bytes 409632 | tf_op jit(solution)/shard_map/all_to_all | solution.py:258
  83.4 0.9 %shard_map.59 = bf16[192,128]{1,0:T(8,128)(2,1)} custom-call(s32[1]{0:T(128)} %bitcast.odd, bf16[8,200,128]{2,1,0:T(8,128)(2,1)S(1)} %all-to-all-done.2.pieces), custom_call_target="tpu_custom_call" | custom-call | tf_op jit(solution)/shard_map/pallas_call | solution.py:260
Async XLA Ops:
  0.7 21.3 %copy-start = (bf16[64,128,128]{2,1,0:T(8,128)(2,1)S(1)}, bf16[64,128,128]{2,1,0:T(8,128)(2,1)}, u32[]{:S(2)}) copy-start(bf16[64,128,128]{2,1,0:T(8,128)(2,1)} %values.3) | copy-start | bytes 6291460
  0.7 21.3 %copy-start.2 = (s32[64,2]{0,1:T(2,128)S(1)}, s32[64,2]{0,1:T(2,128)}, u32[]{:S(2)}) copy-start(s32[64,2]{0,1:T(2,128)} %param.8) | copy-start | bytes 1540
  3.6 20.1 %copy-start.1 = (bf16[128,128]{1,0:T(8,128)(2,1)S(1)}, bf16[128,128]{1,0:T(8,128)(2,1)}, u32[]{:S(2)}) copy-start(bf16[128,128]{1,0:T(8,128)(2,1)} %weight.1) | copy-start | bytes 98308
  20.0 3.7 %collective-permute-start = (bf16[8,216,128]{2,1,0:T(8,128)(2,1)S(1)}, bf16[8,216,128]{2,1,0:T(8,128)(2,1)S(1)}, u32[]{:S(2)}, u32[]{:S(2)}) collective-permute-start(bf16[8,216,128]{2,1,0:T(8,128)(2,1)S(1)} %all_to_all.15.mine), channel_id=1, source_target_pairs={{0,32},{32,0},{64,96},{96,64},{128,160},{160,128},{192,224},{224,1... | collective-permute-start | bytes 1327112 | tf_op jit(solution)/shard_map/ppermute | solution.py:225
  44.6 38.8 %all-to-all-start.2 = ((bf16[8,200,128]{2,1,0:T(8,128)(2,1)}), bf16[8,200,128]{2,1,0:T(8,128)(2,1)S(1)}, u32[]{:S(2)}, u32[]{:S(2)}) async-start(bf16[8,200,128]{2,1,0:T(8,128)(2,1)} %shard_map.58), calls=%async_computation.2 | async-start | bytes 819200 | tf_op jit(solution)/shard_map/all_to_all | solution.py:258

commit v8 on v7

--- a/solution.py
+++ b/solution.py
@@ -24,7 +24,7 @@
 NEAR_ROWS = FAR * OWN + 4 * FAR
 FAR_ROWS = OWN + 8
 
-CHIP_TURN = 7
+CHIP_TURN = 5
 FAR_TURN = 5
 
 

time: 84.7 us -> 84 us (level)
  the two profiles are of different devices: /device:TPU:28 before, /device:TPU:33 now
where the time goes in v8:
time: 84 us; the launch traced here: 83.3 us
  blocking collectives  37.6 us (45%)
  starting transfers between devices  18.7 us (22%)
  waiting for transfers between devices  17.6 us (21%)
  Pallas kernels  8.63 us (10%)
    all_to_all x1, blocking collectives, shards(): lax.all_to_all(partial, ('row', 'col'), 0, 0, axis_index_groups=near_grou...  23.6 us
    all_to_all x1, waiting for transfers between devices, shards(): lax.all_to_all(reduced, 'col', 0, 0, axis_index_groups=FAR_GROUPS, tiled=...  17.6 us
    all_to_all x1, starting transfers between devices, shards(): lax.all_to_all(reduced, 'col', 0, 0, axis_index_groups=FAR_GROUPS, tiled=...  15 us
    all_to_all x1, blocking collectives, shards(): lax.all_to_all(outgoing, 'row', 0, 0, axis_index_groups=CHIP_GROUPS, tile...  14 us
    ppermute x1, starting transfers between devices, shards(): other = lax.ppermute(mine, 'row', [(r, r ^ 1) for r in range(N_ROW)])  3.69 us
    pallas_call x1, Pallas kernels, shards(): pl.pallas_call(column_sums_kernel, out_shape=jax.ShapeDtypeStruct((CHIPS,...  2.74 us
    pallas_call x1, Pallas kernels, shards(): pl.pallas_call(aggregate_kernel, out_shape=jax.ShapeDtypeStruct((NEAR, NE...  2.54 us
  transfers between devices with their start and end apart: 2, of which 1 were waited for; matrix products, arithmetic and copies ran while one was open for 0% of the time, Pallas kernels for 2%

profile of v8, /device:TPU:33, one launch (start us, length us, event | category | flops | bytes accessed | tf_op | source)
XLA Modules:
  0.0 83.3 jit_solution(6365724252235695513)
XLA Ops:
  0.7 0.0 copy-start
  0.7 0.0 copy-start.2
  0.7 2.7 %shard_map.55 = bf16[8,216,128]{2,1,0:T(8,128)(2,1)} custom-call(s32[1]{0:T(128)S(6)} %copy.6.counts_in.counts, s32[2,64]{1,0:T(2,128)} %bitcast.3, bf16[64,128,128]{2,1,0:T(8,128)(2,1)} %values.3, bf16[192,128]{1,0:T(8,128)(2,1)} %features_in.1), custom_call_target="tpu_custom_call" | custom-call | tf_op jit(solution)/shard_map/pallas_call | solution.py:208
  3.4 0.0 copy-start.1
  3.4 14.0 %all_to_all.15.mine = bf16[8,216,128]{2,1,0:T(8,128)(2,1)S(1)} all-to-all(bf16[8,216,128]{2,1,0:T(8,128)(2,1)} %shard_map.55), channel_id=1, replica_groups={{320,384,448,0,64,128,192,256},{352,416,480,32,96,160,224,288},{321,385..., dimensions={0} | all-to-all | bytes 884736 | tf_op jit(solution)/shard_map/all_to_all | solution.py:224
  17.4 3.7 %collective-permute-start = (bf16[8,216,128]{2,1,0:T(8,128)(2,1)S(1)}, bf16[8,216,128]{2,1,0:T(8,128)(2,1)S(1)}, u32[]{:S(2)}, u32[]{:S(2)}) collective-permute-start(bf16[8,216,128]{2,1,0:T(8,128)(2,1)S(1)} %all_to_all.15.mine), channel_id=1, source_target_pairs={{0,32},{32,0},{64,96},{96,64},{128,160},{160,128},{192,224},{224,1... | collective-permute-start | bytes 1327112 | tf_op jit(solution)/shard_map/ppermute | solution.py:225
  21.1 0.0 copy-done
  21.2 0.0 copy-done.2
  21.2 1.5 %shard_map.56.row_sums = bf16[4,32,128]{2,1,0:T(8,128)(2,1)S(1)} custom-call(bf16[8,216,128]{2,1,0:T(8,128)(2,1)S(1)} %all_to_all.15.mine, s32[1]{0:T(128)S(6)} %copy.6.counts_in.counts, s32[2,64]{1,0:T(2,128)S(1)} %bitcast.4, bf16[64,128,128]{2,1,0:T(8,128)(2,1)S(1)} %copy-done), custom_call_target="tpu_custom_call" | custom-call | flops 268435456 | bytes 2097152 | tf_op jit(solution)/shard_map/pallas_call | solution.py:227
  22.7 0.0 collective-permute-done.other
  22.7 0.0 copy-done.1
  22.7 2.5 %shard_map.57 = bf16[4,1568,128]{2,1,0:T(8,128)(2,1)S(1)} custom-call(s32[1]{0:T(128)} %bitcast.1.core, s32[1]{0:T(128)S(6)} %copy.6.counts_in.counts, s32[2,64]{1,0:T(2,128)S(1)} %bitcast.5, bf16[8,216,128]{2,1,0:T(8,128)(2,1)S(1)} %all_to_all.15.mine, bf16[8,216,128]{2,1,0:T(8,128)(2,1)S(1)} %collective-permute-done.other, bf16[128,128]{1,0:T(8,128)(2,1)S(1)} %copy-done.1, ...), custom_call_target="tpu_custom_call" | custom-call | tf_op jit(solution)/shard_map/pallas_call | solution.py:237
  25.2 23.6 %all_to_all.16.pieces = bf16[4,1568,128]{2,1,0:T(8,128)(2,1)S(1)} all-to-all(bf16[4,1568,128]{2,1,0:T(8,128)(2,1)S(1)} %shard_map.57), channel_id=1, replica_groups={{0,1,2,3},{4,5,6,7},{8,9,10,11},{12,13,14,15},{16,17,18,19},{20,21,22,2..., dimensions={0} | all-to-all | bytes 3211264 | tf_op jit(solution)/shard_map/all_to_all | solution.py:249
  48.8 1.0 %shard_map.58 = bf16[8,200,128]{2,1,0:T(8,128)(2,1)} custom-call(bf16[4,1568,128]{2,1,0:T(8,128)(2,1)S(1)} %all_to_all.16.pieces), custom_call_target="tpu_custom_call" | custom-call | tf_op jit(solution)/shard_map/pallas_call | solution.py:251
  49.8 15.0 %all-to-all-start.2 = ((bf16[8,200,128]{2,1,0:T(8,128)(2,1)}), bf16[8,200,128]{2,1,0:T(8,128)(2,1)S(1)}, u32[]{:S(2)}, u32[]{:S(2)}) async-start(bf16[8,200,128]{2,1,0:T(8,128)(2,1)} %shard_map.58), calls=%async_computation.2 | async-start | bytes 819200 | tf_op jit(solution)/shard_map/all_to_all | solution.py:258
  64.8 17.6 %all-to-all-done.2.pieces = bf16[8,200,128]{2,1,0:T(8,128)(2,1)S(1)} async-done(((bf16[8,200,128]{2,1,0:T(8,128)(2,1)}), bf16[8,200,128]{2,1,0:T(8,128)(2,1)S(1)}, u32[]{:S(2)}, u32[]{:S(2)}) %all-to-all-start.2) | async-done | bytes 409632 | tf_op jit(solution)/shard_map/all_to_all | solution.py:258
  82.4 0.9 %shard_map.59 = bf16[192,128]{1,0:T(8,128)(2,1)} custom-call(s32[1]{0:T(128)} %bitcast.odd, bf16[8,200,128]{2,1,0:T(8,128)(2,1)S(1)} %all-to-all-done.2.pieces), custom_call_target="tpu_custom_call" | custom-call | tf_op jit(solution)/shard_map/pallas_call | solution.py:260
Async XLA Ops:
  0.7 20.5 %copy-start = (bf16[64,128,128]{2,1,0:T(8,128)(2,1)S(1)}, bf16[64,128,128]{2,1,0:T(8,128)(2,1)}, u32[]{:S(2)}) copy-start(bf16[64,128,128]{2,1,0:T(8,128)(2,1)} %values.3) | copy-start | bytes 6291460
  0.7 20.5 %copy-start.2 = (s32[64,2]{0,1:T(2,128)S(1)}, s32[64,2]{0,1:T(2,128)}, u32[]{:S(2)}) copy-start(s32[64,2]{0,1:T(2,128)} %param.8) | copy-start | bytes 1540
  3.4 19.3 %copy-start.1 = (bf16[128,128]{1,0:T(8,128)(2,1)S(1)}, bf16[128,128]{1,0:T(8,128)(2,1)}, u32[]{:S(2)}) copy-start(bf16[128,128]{1,0:T(8,128)(2,1)} %weight.1) | copy-start | bytes 98308
  17.4 5.2 %collective-permute-start = (bf16[8,216,128]{2,1,0:T(8,128)(2,1)S(1)}, bf16[8,216,128]{2,1,0:T(8,128)(2,1)S(1)}, u32[]{:S(2)}, u32[]{:S(2)}) collective-permute-start(bf16[8,216,128]{2,1,0:T(8,128)(2,1)S(1)} %all_to_all.15.mine), channel_id=1, source_target_pairs={{0,32},{32,0},{64,96},{96,64},{128,160},{160,128},{192,224},{224,1... | collective-permute-start | bytes 1327112 | tf_op jit(solution)/shard_map/ppermute | solution.py:225
  49.8 32.6 %all-to-all-start.2 = ((bf16[8,200,128]{2,1,0:T(8,128)(2,1)}), bf16[8,200,128]{2,1,0:T(8,128)(2,1)S(1)}, u32[]{:S(2)}, u32[]{:S(2)}) async-start(bf16[8,200,128]{2,1,0:T(8,128)(2,1)} %shard_map.58), calls=%async_computation.2 | async-start | bytes 819200 | tf_op jit(solution)/shard_map/all_to_all | solution.py:258
